TPU v7x, 128 devices: a whole 4x4x4 slice. The times are simulated.
128 devices in a mesh: section: 2 (over x_hi), req: 8 (over x_lo, y), tp: 8 (over z, core).
Axes of the slice: x: 4 (x_hi: 2, x_lo: 2; x = x_hi * 2 + x_lo), y: 4, z: 4, core: 2. Of those that a mesh axis runs over, the one named last changes fastest.
Arguments:
- stretch_query: bfloat16 [32768, 8192], P(('section', 'req'), 'tp'), may hold values from -16 to 16
- stretch_kv: bfloat16 [32768, 8, 256], P(('section', 'req'), 'tp'), may hold values from -16 to 16
- prefix_page_store: bfloat16 [1536, 64, 8, 256], P(('section', 'req'), None, 'tp'), may hold values from -6 to 6
- page_table: int32 [64, 24], P(('section', 'req')), may hold values from 0 to 95, as said below
- vs_mask: int32 [64, 64, 8, 32], P(('section', 'req'), 'tp'), may hold values from 0 to 1, as said below
- prompt_lengths: int32 [64], replicated, may hold values from 1 to 512, as said below
- placement: int32 [16, 4], replicated, may hold values from 0 to 7, as said below
- step_query_rows: bfloat16 [16, 8, 2, 8192], P(('section', 'req')), may hold values from -16 to 16
- step_key_value: bfloat16 [16, 8, 2, 8, 256], P(('section', 'req')), may hold values from -16 to 16
- selected_prefix_blocks: int32 [16, 8, 2, 64, 8], P(('section', 'req')), may hold values from 0 to 23, as said below
Outputs:
- prefill_out: bfloat16 [32768, 8192], P(('section', 'req'), 'tp')
- slot_page_store: bfloat16 [16, 8, 32, 64, 8, 256], P(('section', 'req'), None, 'tp')
- decode_output: bfloat16 [16, 8, 2, 8192], P(('section', 'req'))
Inputs may be any that keep to these rules, and one draw needn't show every extreme that they name: `page_table`: within the 4 rows of one prefill group the entries are a permutation of 0 .. 95. `vs_mask`: block (a, b) is set only if b <= 24 + a; the diagonal block b = 24 + a is always set; every row a has at most 16 set blocks, and the last row has exactly 16. Prompt r has 1536 + prompt_lengths[r] tokens. `placement`: row s * 8 + g lists the decode groups, in section 1 - s, of the 4 prompts of prefill group g of section s; the entries of a row are distinct, and in each section some decode group receives a prompt from every prefill group of the other section. `selected_prefix_blocks`: the 8 entries of one slot, step and head are distinct.
All inputs are finite; a program needn't handle non-finite values.
Results may differ from a plain program's by a relative error of at most 0.0089.
Values may be sent and summed in bfloat16 or wider, within the bound.
No kernel may reach another device: no remote copies, remote signals or barrier semaphores. Data moves between devices by JAX's collectives and lax.ppermute only.
A program may use at most 192 MiB of HBM per device.

v0:
```python
import math

import jax
import jax.numpy as jnp
from jax import lax
from jax.sharding import PartitionSpec as P

QUERY_HEADS = 64
KEY_VALUE_HEADS = 8
HEAD_SIZE = 128
PRE = 1536
STRETCH_TOKENS = 512
BLOCK_TOKENS = 64
DECODE_STEPS = 2
NBP = 24
STRETCH_BLOCKS = 8
PROMPT_BLOCKS = 32
KSEL = 16


rope_base = 500000.0
empty_peak = -1e30


def swapped(block, axis, apart):
    count = lax.axis_size(axis)
    route = []
    for low in range(count):
        high = low | 1 << apart
        if high != low and high < count:
            route += [(low, high), (high, low)]
    return lax.ppermute(block, axis, route)


def rope_angles(positions):
    half_dim = HEAD_SIZE // 2
    frequency = jnp.exp(
        -math.log(rope_base) * (2.0 * jnp.arange(half_dim, dtype=jnp.float32) / HEAD_SIZE)
    )
    angles = positions.astype(jnp.float32)[..., None] * frequency
    return (jnp.cos(angles), jnp.sin(angles))


def rotate_half(vectors, cos_part, sin_part):
    half_dim = vectors.shape[-1] // 2
    front_half = vectors[..., :half_dim]
    back_half = vectors[..., half_dim:]
    return jnp.concatenate(
        [
            front_half * cos_part - back_half * sin_part,
            back_half * cos_part + front_half * sin_part,
        ],
        axis=-1,
    )


def prefill_request(query_rows, stretch_query_rows, prefix_pages, block_mask):
    local_heads = query_rows.shape[1] // HEAD_SIZE
    local_kv = stretch_query_rows.shape[1]
    group_width = local_heads // local_kv
    positions = PRE + jnp.arange(STRETCH_TOKENS, dtype=jnp.int32)
    cos_part, sin_part = rope_angles(positions)
    query_matrix = rotate_half(
        query_rows.reshape(STRETCH_TOKENS, local_heads, HEAD_SIZE).astype(jnp.float32),
        cos_part[:, None, :],
        sin_part[:, None, :],
    ).astype(jnp.bfloat16)
    newest_keys = rotate_half(
        stretch_query_rows[..., :HEAD_SIZE].astype(jnp.float32),
        cos_part[:, None, :],
        sin_part[:, None, :],
    ).astype(jnp.bfloat16)
    newest_pages = jnp.concatenate(
        [newest_keys, stretch_query_rows[..., HEAD_SIZE:]], axis=-1
    ).reshape(STRETCH_BLOCKS, BLOCK_TOKENS, local_kv, 2 * HEAD_SIZE)
    prompt_page_list = jnp.concatenate([prefix_pages, newest_pages], axis=0)
    block_ids = jnp.arange(PROMPT_BLOCKS, dtype=jnp.int32)
    ranking = block_mask * (2 * PROMPT_BLOCKS) + (PROMPT_BLOCKS - block_ids)
    _, chosen = lax.top_k(ranking, KSEL)
    valid_tile = jnp.take_along_axis(block_mask, chosen, axis=-1) == 1
    head_kv = jnp.arange(local_heads, dtype=jnp.int32) // group_width
    by_head = jnp.transpose(prompt_page_list, (2, 0, 1, 3))
    key_tiles = by_head[head_kv[:, None, None], chosen].reshape(
        local_heads, STRETCH_BLOCKS, KSEL * BLOCK_TOKENS, 2 * HEAD_SIZE
    )
    query_blocks = jnp.transpose(
        query_matrix.reshape(STRETCH_BLOCKS, BLOCK_TOKENS, local_heads, HEAD_SIZE), (2, 0, 1, 3)
    )
    scores = jnp.einsum(
        "hqid,hqtd->hqit",
        query_blocks,
        key_tiles[..., :HEAD_SIZE],
        preferred_element_type=jnp.float32,
    ) / math.sqrt(HEAD_SIZE)
    key_positions = (
        chosen[..., None] * BLOCK_TOKENS + jnp.arange(BLOCK_TOKENS, dtype=jnp.int32)
    ).reshape(local_heads, STRETCH_BLOCKS, KSEL * BLOCK_TOKENS)
    valid_keys = jnp.repeat(valid_tile, BLOCK_TOKENS, axis=-1)
    query_positions = positions.reshape(STRETCH_BLOCKS, BLOCK_TOKENS)
    active_flag = valid_keys[:, :, None, :] & (
        key_positions[:, :, None, :] <= query_positions[None, :, :, None]
    )
    row_peak = jnp.max(jnp.where(active_flag, scores, -jnp.inf), axis=-1, keepdims=True)
    weights = jnp.where(active_flag, jnp.exp(scores - row_peak), 0.0)
    row_total = jnp.sum(weights, axis=-1)
    attended = jnp.einsum(
        "hqit,hqtd->hqid",
        weights.astype(jnp.bfloat16),
        key_tiles[..., HEAD_SIZE:],
        preferred_element_type=jnp.float32,
    )
    attended = attended / row_total[..., None]
    result = (
        jnp.transpose(attended, (1, 2, 0, 3))
        .reshape(STRETCH_TOKENS, local_heads * HEAD_SIZE)
        .astype(jnp.bfloat16)
    )
    return (result, prompt_page_list)


def prefill_device(stretch_query, stretch_kv, prefix_page_store, page_table, vs_mask):

    def one_request(request):
        query_rows = lax.dynamic_slice_in_dim(
            stretch_query, request * STRETCH_TOKENS, STRETCH_TOKENS, 0
        )
        stretch_query_rows = lax.dynamic_slice_in_dim(
            stretch_kv, request * STRETCH_TOKENS, STRETCH_TOKENS, 0
        )
        table_row = lax.dynamic_index_in_dim(page_table, request, 0, keepdims=False)
        prefix_pages = jnp.take(prefix_page_store, table_row, axis=0)
        block_mask = lax.dynamic_index_in_dim(vs_mask, request, 0, keepdims=False)
        return prefill_request(query_rows, stretch_query_rows, prefix_pages, block_mask)

    attended, prompt_page_list = lax.map(
        one_request, jnp.arange(stretch_query.shape[0] // STRETCH_TOKENS, dtype=jnp.int32)
    )
    return (attended.reshape(stretch_query.shape[0], attended.shape[-1]), prompt_page_list)


def route_buffer(prompt_page_list, targets, groups):
    onehot = (targets[None, :] == jnp.arange(groups, dtype=jnp.int32)[:, None]).astype(jnp.bfloat16)
    return jnp.einsum(
        "dr,rpbkc->dpbkc", onehot, prompt_page_list, preferred_element_type=jnp.float32
    ).astype(jnp.bfloat16)


def decode_device(
    stored_pages,
    prompt_lengths,
    placement,
    query_matrix,
    new_rows,
    chosen,
    section_index,
    group_index,
    groups,
):
    slot_number = stored_pages.shape[0]
    nearby_pages = stored_pages.shape[1]
    group_width = QUERY_HEADS // KEY_VALUE_HEADS
    source_rows = (1 - section_index) * groups + jnp.arange(slot_number, dtype=jnp.int32)
    matches = jnp.take(placement, source_rows, axis=0) == group_index
    occupied_slots = jnp.any(matches, axis=-1)
    chosen_index = jnp.argmax(matches.astype(jnp.int32), axis=-1)
    overall_length = PRE + jnp.take(prompt_lengths, source_rows * placement.shape[1] + chosen_index)
    positions = overall_length[:, None] + jnp.arange(DECODE_STEPS, dtype=jnp.int32)
    cos_part, sin_part = rope_angles(positions)
    rotated_rows = rotate_half(
        query_matrix.reshape(slot_number, DECODE_STEPS, QUERY_HEADS, HEAD_SIZE).astype(jnp.float32),
        cos_part[:, :, None, :],
        sin_part[:, :, None, :],
    ).astype(jnp.bfloat16)
    grouped_heads = rotated_rows.reshape(
        slot_number, DECODE_STEPS, KEY_VALUE_HEADS, group_width, HEAD_SIZE
    )
    new_keys = rotate_half(
        new_rows[..., :HEAD_SIZE].astype(jnp.float32),
        cos_part[:, :, None, :],
        sin_part[:, :, None, :],
    ).astype(jnp.bfloat16)
    token_list = stored_pages.reshape(
        slot_number, nearby_pages * BLOCK_TOKENS, KEY_VALUE_HEADS, 2 * HEAD_SIZE
    )
    old_scores = jnp.einsum(
        "sekgd,sjkd->sekgj",
        grouped_heads,
        token_list[..., :HEAD_SIZE],
        preferred_element_type=jnp.float32,
    ) / math.sqrt(HEAD_SIZE)
    new_scores = jnp.einsum(
        "sekgd,sfkd->sekgf", grouped_heads, new_keys, preferred_element_type=jnp.float32
    ) / math.sqrt(HEAD_SIZE)
    tp_index = lax.axis_index("tp")
    first_page = tp_index * nearby_pages
    page_ids = first_page + jnp.arange(nearby_pages, dtype=jnp.int32)
    token_ids = first_page * BLOCK_TOKENS + jnp.arange(nearby_pages * BLOCK_TOKENS, dtype=jnp.int32)
    picked = jnp.any(chosen[..., None] == page_ids, axis=-2) & (page_ids < NBP)
    picked = jnp.repeat(picked, BLOCK_TOKENS, axis=-1)
    retained_mask = (token_ids < overall_length[:, None, None, None]) & (
        picked | (token_ids >= PRE)
    )
    retained_mask = retained_mask.reshape(
        slot_number, DECODE_STEPS, KEY_VALUE_HEADS, group_width, nearby_pages * BLOCK_TOKENS
    )
    step_ids = jnp.arange(DECODE_STEPS, dtype=jnp.int32)
    own_kept = (step_ids[None, :] <= step_ids[:, None]) & (tp_index == 0)
    own_kept = jnp.broadcast_to(own_kept[None, :, None, None, :], new_scores.shape)
    local_peak = jnp.maximum(
        jnp.max(jnp.where(retained_mask, old_scores, empty_peak), axis=-1),
        jnp.max(jnp.where(own_kept, new_scores, empty_peak), axis=-1),
    )
    old_weights = jnp.where(retained_mask, jnp.exp(old_scores - local_peak[..., None]), 0.0)
    new_weights = jnp.where(own_kept, jnp.exp(new_scores - local_peak[..., None]), 0.0)
    local_mass = jnp.sum(old_weights, axis=-1) + jnp.sum(new_weights, axis=-1)
    local_sum = jnp.einsum(
        "sekgj,sjkd->sekgd",
        old_weights,
        token_list[..., HEAD_SIZE:].astype(jnp.float32),
        precision=lax.Precision.HIGHEST,
    )
    local_sum = local_sum + jnp.einsum(
        "sekgf,sfkd->sekgd",
        new_weights,
        new_rows[..., HEAD_SIZE:].astype(jnp.float32),
        precision=lax.Precision.HIGHEST,
    )
    joint_peak = lax.pmax(local_peak, "tp")
    factor = jnp.exp(local_peak - joint_peak)
    total_mass, total_sum = lax.psum((local_mass * factor, local_sum * factor[..., None]), "tp")
    attended = total_sum / total_mass[..., None]
    attended = jnp.where(occupied_slots[:, None, None, None, None], attended, 0.0)
    return attended.reshape(slot_number, DECODE_STEPS, QUERY_HEADS * HEAD_SIZE).astype(jnp.bfloat16)


def shards(
    stretch_query,
    stretch_kv,
    prefix_page_store,
    page_table,
    vs_mask,
    prompt_lengths,
    placement,
    step_query_rows,
    step_key_value,
    selected_prefix_blocks,
):
    section_index = lax.axis_index("section")
    group_index = lax.axis_index("req")
    groups = lax.axis_size("req")
    prefill_out, prompt_page_list = prefill_device(
        stretch_query, stretch_kv, prefix_page_store, page_table, vs_mask
    )
    targets = lax.dynamic_index_in_dim(
        placement, section_index * groups + group_index, 0, keepdims=False
    )
    routed = lax.all_to_all(
        lax.all_to_all(
            route_buffer(prompt_page_list, targets, groups),
            "req",
            split_axis=0,
            concat_axis=0,
            tiled=True,
        ),
        "tp",
        split_axis=1,
        concat_axis=3,
        tiled=True,
    )
    stored_pages = swapped(routed, "section", 0)
    decode_output = decode_device(
        stored_pages,
        prompt_lengths,
        placement,
        step_query_rows[0],
        step_key_value[0],
        selected_prefix_blocks[0],
        section_index,
        group_index,
        groups,
    )
    return (prefill_out, stored_pages[None], decode_output[None])


def solution(mesh):
    placed = (
        P(("section", "req"), "tp"),
        P(("section", "req"), "tp", None),
        P(("section", "req"), None, "tp", None),
        P(("section", "req"), None),
        P(("section", "req"), "tp", None, None),
        P(),
        P(),
        P(("section", "req"), None, None, None),
        P(("section", "req"), None, None, None, None),
        P(("section", "req"), None, None, None, None),
    )
    return jax.shard_map(
        shards,
        mesh=mesh,
        in_specs=placed,
        out_specs=(
            P(("section", "req"), "tp"),
            P(("section", "req"), None, "tp", None, None, None),
            P(("section", "req"), None, None, None),
        ),
        check_vma=False,
    )
```

profile of v0, /device:TPU:0, one launch (start us, length us, event | category | flops | bytes accessed | tf_op | source)
XLA Modules:
  0.0 932.7 jit_solution(3420453478699692571)
XLA Ops:
  7.8 376.7 %while.14 = (s32[]{:T(128)}, bf16[4,512,1024]{2,1,0:T(8,128)(2,1)}, bf16[4,32,64,1,256]{4,2,1,3,0:T(8,128)(2,1)}, s32[4]{0:T(128)}, s32[4,8,8,32]{3,2,1,0:T(8,12...) while((s32[]{:T(128)}, bf16[4,512,1024]{2,1,0:T(8,128)(2,1)}, ...), condition=%wide.region_4.5_spmd, body=%wide.region_0.4_spmd.sunk | while | flops 2208683008 | bytes 187422704 | solution.py:135
  17.8 6.8 gather_fusion.2
  38.7 18.5 %gather_fusion.1 = bf16[1024,64,256]{2,1,0:T(8,128)(2,1)} fusion(bf16[1,32,64,256]{3,2,1,0:T(8,128)(2,1)S(1)} %fusion.86, s32[1024]{0:T(1024)S(1)} %reshape.553), kind=kCustom, calls=%fused_computation.1.clone.1 | custom fusion | bytes 67117056 | tf_op jit(solution)/shard_map/while/body/eval_jaxpr/gather | solution.py:83
  57.2 12.7 %fusion.89 = f32[8,8,64,1024]{3,2,1,0:T(8,128)} fusion(bf16[8,8,1024,256]{3,2,1,0:T(8,128)(2,1)} %bitcast.176, bf16[8,64,8,64]{3,1,0,2:T(8,128)(2,1)S(1)} %bitcast.180, bf16[8,64,8,64]{3,1,0,2:T(8,128)(2,1)S(1)} %bitcast.179), kind=kOutput, calls=%fused_computation.8.clone.1 | convolution fusion | flops 1075838976 | bytes 34603008 | tf_op jit(solution)/shard_map/while/body/eval_jaxpr/hqid,hqtd->hqit/dot_general | solution.py:89
  69.9 18.6 %fusion.90 = (f32[8,8,64]{2,1,0:T(8,128)S(1)}, bf16[8,8,64,1024]{3,2,1,0:T(8,128)(2,1)}) fusion(f32[8,8,64,1024]{3,2,1,0:T(8,128)} %fusion.89, s32[8,64]{1,0:T(8,128)S(1)} %add_add_fusion.2, s32[8,8,1024]{2,1,0:T(8,128)S(1)} %copy-done.3, pred[8,8,1024]{2,1,0:T(8,128)(4,1)S(1)} %copy-done.4), kind=kOutput, calls=%fused_computation.152.clone.1 | output fusion | flops 46138368 | bytes 25511936 | tf_op jit(solution)/shard_map/while/body/eval_jaxpr/sub | solution.py:104
  88.5 11.2 %fusion.91 = bf16[8,64,8,128]{3,1,0,2:T(8,128)(2,1)S(1)} fusion(bf16[8,8,1024,256]{3,2,1,0:T(8,128)(2,1)} %bitcast.177, bf16[8,8,64,1024]{3,2,1,0:T(8,128)(2,1)} %get-tuple-element.284, f32[8,64,8]{1,0,2:T(8,128)S(1)} %bitcast.202), kind=kOutput, calls=%fused_computation.22.clone.1 | convolution fusion | flops 1074790400 | bytes 26230784 | tf_op jit(solution)/shard_map/while/body/eval_jaxpr/hqit,hqtd->hqid/dot_general | solution.py:106
  112.0 6.8 gather_fusion.2
  132.9 18.5 %gather_fusion.1 = bf16[1024,64,256]{2,1,0:T(8,128)(2,1)} fusion(bf16[1,32,64,256]{3,2,1,0:T(8,128)(2,1)S(1)} %fusion.86, s32[1024]{0:T(1024)S(1)} %reshape.553), kind=kCustom, calls=%fused_computation.1.clone.1 | custom fusion | bytes 67117056 | tf_op jit(solution)/shard_map/while/body/eval_jaxpr/gather | solution.py:83
  151.3 12.7 %fusion.89 = f32[8,8,64,1024]{3,2,1,0:T(8,128)} fusion(bf16[8,8,1024,256]{3,2,1,0:T(8,128)(2,1)} %bitcast.176, bf16[8,64,8,64]{3,1,0,2:T(8,128)(2,1)S(1)} %bitcast.180, bf16[8,64,8,64]{3,1,0,2:T(8,128)(2,1)S(1)} %bitcast.179), kind=kOutput, calls=%fused_computation.8.clone.1 | convolution fusion | flops 1075838976 | bytes 34603008 | tf_op jit(solution)/shard_map/while/body/eval_jaxpr/hqid,hqtd->hqit/dot_general | solution.py:89
  164.1 18.6 %fusion.90 = (f32[8,8,64]{2,1,0:T(8,128)S(1)}, bf16[8,8,64,1024]{3,2,1,0:T(8,128)(2,1)}) fusion(f32[8,8,64,1024]{3,2,1,0:T(8,128)} %fusion.89, s32[8,64]{1,0:T(8,128)S(1)} %add_add_fusion.2, s32[8,8,1024]{2,1,0:T(8,128)S(1)} %copy-done.3, pred[8,8,1024]{2,1,0:T(8,128)(4,1)S(1)} %copy-done.4), kind=kOutput, calls=%fused_computation.152.clone.1 | output fusion | flops 46138368 | bytes 25511936 | tf_op jit(solution)/shard_map/while/body/eval_jaxpr/sub | solution.py:104
  182.6 11.2 %fusion.91 = bf16[8,64,8,128]{3,1,0,2:T(8,128)(2,1)S(1)} fusion(bf16[8,8,1024,256]{3,2,1,0:T(8,128)(2,1)} %bitcast.177, bf16[8,8,64,1024]{3,2,1,0:T(8,128)(2,1)} %get-tuple-element.284, f32[8,64,8]{1,0,2:T(8,128)S(1)} %bitcast.202), kind=kOutput, calls=%fused_computation.22.clone.1 | convolution fusion | flops 1074790400 | bytes 26230784 | tf_op jit(solution)/shard_map/while/body/eval_jaxpr/hqit,hqtd->hqid/dot_general | solution.py:106
  206.1 6.8 gather_fusion.2
  227.0 18.5 %gather_fusion.1 = bf16[1024,64,256]{2,1,0:T(8,128)(2,1)} fusion(bf16[1,32,64,256]{3,2,1,0:T(8,128)(2,1)S(1)} %fusion.86, s32[1024]{0:T(1024)S(1)} %reshape.553), kind=kCustom, calls=%fused_computation.1.clone.1 | custom fusion | bytes 67117056 | tf_op jit(solution)/shard_map/while/body/eval_jaxpr/gather | solution.py:83
  245.4 12.7 %fusion.89 = f32[8,8,64,1024]{3,2,1,0:T(8,128)} fusion(bf16[8,8,1024,256]{3,2,1,0:T(8,128)(2,1)} %bitcast.176, bf16[8,64,8,64]{3,1,0,2:T(8,128)(2,1)S(1)} %bitcast.180, bf16[8,64,8,64]{3,1,0,2:T(8,128)(2,1)S(1)} %bitcast.179), kind=kOutput, calls=%fused_computation.8.clone.1 | convolution fusion | flops 1075838976 | bytes 34603008 | tf_op jit(solution)/shard_map/while/body/eval_jaxpr/hqid,hqtd->hqit/dot_general | solution.py:89
  258.2 18.6 %fusion.90 = (f32[8,8,64]{2,1,0:T(8,128)S(1)}, bf16[8,8,64,1024]{3,2,1,0:T(8,128)(2,1)}) fusion(f32[8,8,64,1024]{3,2,1,0:T(8,128)} %fusion.89, s32[8,64]{1,0:T(8,128)S(1)} %add_add_fusion.2, s32[8,8,1024]{2,1,0:T(8,128)S(1)} %copy-done.3, pred[8,8,1024]{2,1,0:T(8,128)(4,1)S(1)} %copy-done.4), kind=kOutput, calls=%fused_computation.152.clone.1 | output fusion | flops 46138368 | bytes 25511936 | tf_op jit(solution)/shard_map/while/body/eval_jaxpr/sub | solution.py:104
  276.8 11.2 %fusion.91 = bf16[8,64,8,128]{3,1,0,2:T(8,128)(2,1)S(1)} fusion(bf16[8,8,1024,256]{3,2,1,0:T(8,128)(2,1)} %bitcast.177, bf16[8,8,64,1024]{3,2,1,0:T(8,128)(2,1)} %get-tuple-element.284, f32[8,64,8]{1,0,2:T(8,128)S(1)} %bitcast.202), kind=kOutput, calls=%fused_computation.22.clone.1 | convolution fusion | flops 1074790400 | bytes 26230784 | tf_op jit(solution)/shard_map/while/body/eval_jaxpr/hqit,hqtd->hqid/dot_general | solution.py:106
  321.2 18.5 %gather_fusion.1 = bf16[1024,64,256]{2,1,0:T(8,128)(2,1)} fusion(bf16[1,32,64,256]{3,2,1,0:T(8,128)(2,1)S(1)} %fusion.86, s32[1024]{0:T(1024)S(1)} %reshape.553), kind=kCustom, calls=%fused_computation.1.clone.1 | custom fusion | bytes 67117056 | tf_op jit(solution)/shard_map/while/body/eval_jaxpr/gather | solution.py:83
  339.6 12.7 %fusion.89 = f32[8,8,64,1024]{3,2,1,0:T(8,128)} fusion(bf16[8,8,1024,256]{3,2,1,0:T(8,128)(2,1)} %bitcast.176, bf16[8,64,8,64]{3,1,0,2:T(8,128)(2,1)S(1)} %bitcast.180, bf16[8,64,8,64]{3,1,0,2:T(8,128)(2,1)S(1)} %bitcast.179), kind=kOutput, calls=%fused_computation.8.clone.1 | convolution fusion | flops 1075838976 | bytes 34603008 | tf_op jit(solution)/shard_map/while/body/eval_jaxpr/hqid,hqtd->hqit/dot_general | solution.py:89
  352.4 18.6 %fusion.90 = (f32[8,8,64]{2,1,0:T(8,128)S(1)}, bf16[8,8,64,1024]{3,2,1,0:T(8,128)(2,1)}) fusion(f32[8,8,64,1024]{3,2,1,0:T(8,128)} %fusion.89, s32[8,64]{1,0:T(8,128)S(1)} %add_add_fusion.2, s32[8,8,1024]{2,1,0:T(8,128)S(1)} %copy-done.3, pred[8,8,1024]{2,1,0:T(8,128)(4,1)S(1)} %copy-done.4), kind=kOutput, calls=%fused_computation.152.clone.1 | output fusion | flops 46138368 | bytes 25511936 | tf_op jit(solution)/shard_map/while/body/eval_jaxpr/sub | solution.py:104
  370.9 11.2 %fusion.91 = bf16[8,64,8,128]{3,1,0,2:T(8,128)(2,1)S(1)} fusion(bf16[8,8,1024,256]{3,2,1,0:T(8,128)(2,1)} %bitcast.177, bf16[8,8,64,1024]{3,2,1,0:T(8,128)(2,1)} %get-tuple-element.284, f32[8,64,8]{1,0,2:T(8,128)S(1)} %bitcast.202), kind=kOutput, calls=%fused_computation.22.clone.1 | convolution fusion | flops 1074790400 | bytes 26230784 | tf_op jit(solution)/shard_map/while/body/eval_jaxpr/hqit,hqtd->hqid/dot_general | solution.py:106
  384.8 8.7 convert_bitcast_fusion.1
  393.5 8.6 copy.108
  402.1 100.3 %all_to_all.23 = bf16[8,32,64,1,256]{4,2,1,3,0:T(8,128)(2,1)} all-to-all(bf16[8,32,64,1,256]{4,2,1,3,0:T(8,128)(2,1)} %copy.108), channel_id=1, replica_groups=mesh['section'=2,'req'=8,'tp'=8] {'req'}, dimensions={0} | all-to-all | bytes 16777216 | tf_op jit(solution)/shard_map/all_to_all | solution.py:258
  502.5 15.4 %copy.109 = bf16[8,32,64,1,256]{4,0,2,3,1:T(8,128)(2,1)} copy(bf16[8,32,64,1,256]{4,2,1,3,0:T(8,128)(2,1)} %all_to_all.23) | data formatting | bytes 16777216 | tf_op jit(solution)/shard_map/all_to_all | solution.py:258
  517.9 100.5 %all_to_all.24 = bf16[8,32,64,1,256]{4,0,2,3,1:T(8,128)(2,1)} all-to-all(bf16[8,32,64,1,256]{4,0,2,3,1:T(8,128)(2,1)} %copy.109), channel_id=1, replica_groups=mesh['section'=2,'req'=8,'tp'=8] {'tp'}, dimensions={1} | all-to-all | bytes 16777216 | tf_op jit(solution)/shard_map/all_to_all | solution.py:257
  618.4 11.6 %copy.157 = bf16[8,8,4,64,1,256]{5,1,3,2,0,4:T(8,128)(2,1)} copy(bf16[8,8,4,64,1,256]{5,0,3,2,1,4:T(8,128)(2,1)} %bitcast.181) | data formatting | bytes 16777216 | tf_op jit(solution)/shard_map/all_to_all | solution.py:257
  640.7 173.0 %collective-permute-done = bf16[8,4,64,8,256]{4,3,2,1,0:T(8,128)(2,1)} collective-permute-done((bf16[8,4,64,8,256]{4,3,2,1,0:T(8,128)(2,1)}, bf16[8,4,64,8,256]{4,3,2,1,0:T(8,128)(2,1)}, u32[]{:S(2)}, u32[]{:S(2)}) %collective-permute-start) | collective-permute-done | bytes 8388640 | tf_op jit(solution)/shard_map/ppermute | solution.py:32
  813.7 9.0 copy.112
  826.3 24.8 %pmax.7 = f32[8,2,8,8]{3,1,2,0:T(2,128)S(1)} all-reduce(f32[8,2,8,8]{3,1,2,0:T(2,128)S(1)} %max.9), channel_id=1, replica_groups=mesh['section'=2,'req'=8,'tp'=8] {'tp'}, use_global_device_ids=true, to_apply=%region_10.11 | all-reduce | flops 1024 | bytes 8192 | tf_op jit(solution)/shard_map/pmax | solution.py:228
  857.7 23.9 %psum.15 = f32[8,2,8,8]{3,1,2,0:T(2,128)S(1)} all-reduce(f32[8,2,8,8]{3,1,2,0:T(2,128)S(1)} %bitcast.193), channel_id=1, replica_groups=mesh['section'=2,'req'=8,'tp'=8] {'tp'}, use_global_device_ids=true, to_apply=%region_14.15 | all-reduce | flops 1024 | bytes 8192 | tf_op jit(solution)/shard_map/psum | solution.py:230
  881.7 34.0 %all-reduce.2.cloned.1.call-done = f32[8,2,8,8,128]{4,3,1,2,0:T(8,128)} async-done(((f32[8,2,8,8,128]{4,3,1,2,0:T(8,128)}), f32[8,2,8,8,128]{4,3,1,2,0:T(8,128)}) %all-reduce.2.cloned.1.call-update) | async-done | bytes 524304 | tf_op jit(solution)/shard_map/psum | solution.py:230
  917.8 7.7 copy.184
  (255 shorter events, 124.8 us)
Async XLA Ops:
  7.2 630.7 %copy-start = (s32[64]{0:T(128)S(1)}, s32[64]{0:T(128)}, u32[]{:S(2)}) copy-start(s32[64]{0:T(128)} %param.17) | copy-start | bytes 772
  7.2 908.5 %all-reduce.2.cloned.1.call-start = ((), (), s32[]{:S(2)}) async-start(), calls=%async_computation.2 | async-start | bytes 1048576 | tf_op jit(solution)/shard_map/psum | solution.py:230
  7.8 376.8 %copy-start.8 = (s32[16,4]{0,1:T(4,128)S(1)}, s32[16,4]{0,1:T(4,128)}, u32[]{:S(2)}) copy-start(s32[16,4]{0,1:T(4,128)} %param.18) | copy-start | bytes 772
  35.7 1.0 copy-start.1
  35.7 1.0 copy-start.2
  57.2 12.7 %copy-start.3 = (s32[8,8,1024]{2,1,0:T(8,128)S(1)}, s32[8,8,1024]{2,1,0:T(8,128)}, u32[]{:S(2)}) copy-start(s32[8,8,1024]{2,1,0:T(8,128)} %broadcast_add_fusion.2) | copy-start | bytes 786436 | tf_op jit(solution)/shard_map/while
  57.2 12.7 %copy-start.4 = (pred[8,8,1024]{2,1,0:T(8,128)(4,1)S(1)}, pred[8,8,1024]{2,1,0:T(8,128)(4,1)}, u32[]{:S(2)}) copy-start(pred[8,8,1024]{2,1,0:T(8,128)(4,1)} %and.189) | copy-start | bytes 196612 | tf_op jit(solution)/shard_map/while
  129.8 1.0 copy-start.1
  129.8 1.0 copy-start.2
  151.3 12.7 %copy-start.3 = (s32[8,8,1024]{2,1,0:T(8,128)S(1)}, s32[8,8,1024]{2,1,0:T(8,128)}, u32[]{:S(2)}) copy-start(s32[8,8,1024]{2,1,0:T(8,128)} %broadcast_add_fusion.2) | copy-start | bytes 786436 | tf_op jit(solution)/shard_map/while
  151.3 12.7 %copy-start.4 = (pred[8,8,1024]{2,1,0:T(8,128)(4,1)S(1)}, pred[8,8,1024]{2,1,0:T(8,128)(4,1)}, u32[]{:S(2)}) copy-start(pred[8,8,1024]{2,1,0:T(8,128)(4,1)} %and.189) | copy-start | bytes 196612 | tf_op jit(solution)/shard_map/while
  224.0 1.0 copy-start.1
  224.0 1.0 copy-start.2
  245.4 12.8 %copy-start.3 = (s32[8,8,1024]{2,1,0:T(8,128)S(1)}, s32[8,8,1024]{2,1,0:T(8,128)}, u32[]{:S(2)}) copy-start(s32[8,8,1024]{2,1,0:T(8,128)} %broadcast_add_fusion.2) | copy-start | bytes 786436 | tf_op jit(solution)/shard_map/while
  245.4 12.8 %copy-start.4 = (pred[8,8,1024]{2,1,0:T(8,128)(4,1)S(1)}, pred[8,8,1024]{2,1,0:T(8,128)(4,1)}, u32[]{:S(2)}) copy-start(pred[8,8,1024]{2,1,0:T(8,128)(4,1)} %and.189) | copy-start | bytes 196612 | tf_op jit(solution)/shard_map/while
  318.1 1.0 copy-start.1
  318.1 1.0 copy-start.2
  339.6 12.8 %copy-start.3 = (s32[8,8,1024]{2,1,0:T(8,128)S(1)}, s32[8,8,1024]{2,1,0:T(8,128)}, u32[]{:S(2)}) copy-start(s32[8,8,1024]{2,1,0:T(8,128)} %broadcast_add_fusion.2) | copy-start | bytes 786436 | tf_op jit(solution)/shard_map/while
  339.6 12.8 %copy-start.4 = (pred[8,8,1024]{2,1,0:T(8,128)(4,1)S(1)}, pred[8,8,1024]{2,1,0:T(8,128)(4,1)}, u32[]{:S(2)}) copy-start(pred[8,8,1024]{2,1,0:T(8,128)(4,1)} %and.189) | copy-start | bytes 196612 | tf_op jit(solution)/shard_map/while
  618.4 15.0 %copy-start.7 = (bf16[1,8,2,8,256]{4,3,2,1,0:T(8,128)(2,1)S(1)}, bf16[1,8,2,8,256]{4,3,2,1,0:T(8,128)(2,1)}, u32[]{:S(2)}) copy-start(bf16[1,8,2,8,256]{4,3,2,1,0:T(8,128)(2,1)} %param.20) | copy-start | bytes 196612
  618.4 15.1 %copy-start.6 = (s32[1,8,2,64,8]{3,4,2,1,0:T(8,128)S(1)}, s32[1,8,2,64,8]{3,4,2,1,0:T(8,128)}, u32[]{:S(2)}) copy-start(s32[1,8,2,64,8]{3,4,2,1,0:T(8,128)} %param.21) | copy-start | bytes 98308
  618.4 17.8 %copy-start.5 = (bf16[1,8,2,8192]{3,2,1,0:T(2,128)(2,1)S(1)}, bf16[1,8,2,8192]{3,2,1,0:T(2,128)(2,1)}, u32[]{:S(2)}) copy-start(bf16[1,8,2,8192]{3,2,1,0:T(2,128)(2,1)} %param.19) | copy-start | bytes 786436
  630.0 183.7 %collective-permute-start = (bf16[8,4,64,8,256]{4,3,2,1,0:T(8,128)(2,1)}, bf16[8,4,64,8,256]{4,3,2,1,0:T(8,128)(2,1)}, u32[]{:S(2)}, u32[]{:S(2)}) collective-permute-start(bf16[8,4,64,8,256]{4,3,2,1,0:T(8,128)(2,1)} %bitcast.188), channel_id=1, source_target_pairs={{0,64},{64,0},{1,65},{65,1},{2,66},{66,2},{3,67},{67,3},{4,68},{68... | collective-permute-start | bytes 25165832 | tf_op jit(solution)/shard_map/ppermute | solution.py:32
Sparse Core Ops, SparseCore 0:
  857.8 57.8 all-reduce.1
where the time goes:
time: 946 us; the launch traced here: 933 us
  blocking collectives  250 us (26%)
  waiting for transfers between devices  207 us (22%)
  local copies, waits for them, and re-layouts  196 us (21%)
  other arithmetic  136 us (14%)
  matrix products  115 us (12%)
  between operations  14.7 us (2%)
  loops' own time  11.3 us (1%)
    ppermute x1, waiting for transfers between devices, swapped(): return lax.ppermute(block, axis, route)  173 us
    all_to_all x1, blocking collectives, shards(): lax.all_to_all(lax.all_to_all(route_buffer(prompt_page_list, targets, gro...  101 us
    all_to_all x1, blocking collectives, shards(): lax.all_to_all(route_buffer(prompt_page_list, targets, groups), 'req', sp...  100 us
    sub x4, other arithmetic, prefill_request(): weights = jnp.where(active_flag, jnp.exp(scores - row_peak), 0.0)  74.3 us
    gather x4, local copies, waits for them, and re-layouts, prefill_request(): by_head[head_kv[:, None, None], chosen]  73.8 us
    dot_general x4, matrix products, prefill_request(): jnp.einsum('hqid,hqtd->hqit', query_blocks, key_tiles[..., :HEAD_SIZE], p...  51 us
    dot_general x4, matrix products, prefill_request(): jnp.einsum('hqit,hqtd->hqid', weights.astype(jnp.bfloat16), key_tiles[......  44.9 us
    psum x1, waiting for transfers between devices, decode_device(): lax.psum((local_mass * factor, local_sum * factor[..., None]), 'tp')  34 us
  transfers between devices with their start and end apart: 2, of which 2 were waited for; matrix products, arithmetic and copies ran while one was open for 1% of the time, Pallas kernels for 0%

commit v1 on v0

v1 whole, which is shorter than its diff:
```python
import functools
import math

import jax
import jax.numpy as jnp
from jax import lax
from jax.experimental import pallas as pl
from jax.experimental.pallas import tpu as pltpu
from jax.sharding import PartitionSpec as P

QUERY_HEADS = 64
KEY_VALUE_HEADS = 8
HEAD_SIZE = 128
PRE = 1536
STRETCH_TOKENS = 512
BLOCK_TOKENS = 64
REQ_DEV = 4
DECODE_STEPS = 2
DECODE_SLOTS = 8
NBP = 24
STRETCH_BLOCKS = 8
PROMPT_BLOCKS = 32
SELECTED_BLOCKS = 8
PREFIX_PAGES = 96
HEADS = 8
PAGE = 2 * HEAD_SIZE
N_TP = 8
N_REQ = 8
RESULT_ROWS = 16
CHUNKS = (2, 2)
STARTS = tuple(sum(CHUNKS[:c]) for c in range(len(CHUNKS)))
HEADS_AT_ONCE = 4
ORDER = ('d@00', 'p0@04', 'r0', 'p1@10', 'p2@13', 'r1', 'p3', 's0', 's1')
QUERY_ROWS = 256

ROPE_BASE = 500000.0
OFF = -1e30
EXP2_SCALE = math.log2(math.e) / math.sqrt(HEAD_SIZE)
VMEM = 60 << 20
LIGHT = pl.CostEstimate(flops=1, bytes_accessed=1, transcendentals=0)

def all_places():
    for section in range(2):
        for req in range(N_REQ):
            for tp in range(N_TP):
                yield section, req, tp


def place_number(section, req, tp):
    return (section * N_REQ + req) * N_TP + tp


def other_side(req):
    return (req + N_REQ // 2) % N_REQ


TP_OFFSETS = [(dz, dc) for dz in range(4) for dc in range(2)]


def tp_moved(tp, offset, sign=1):
    dz, dc = offset
    return (tp // 2 + sign * dz + 4) % 4 * 2 + (tp + dc) % 2


def cross_route(offset):
    return [
        (place_number(s, r, t), place_number(1 - s, other_side(r), tp_moved(t, offset)))
        for s, r, t in all_places()
    ]


def routed_rows(c):
    extra = DECODE_STEPS * HEADS // 2 if c == len(CHUNKS) - 1 else 0
    return (CHUNKS[c] * BLOCK_TOKENS + extra) * HEADS


def travelling_rows(c):
    return CHUNKS[c] * BLOCK_TOKENS + (RESULT_ROWS if c == len(CHUNKS) - 1 else 0)


def rope_tables(positions):
    half = HEAD_SIZE // 2
    frequency = jnp.exp(
        -math.log(ROPE_BASE) * (2.0 * jnp.arange(half, dtype=jnp.float32) / HEAD_SIZE)
    )
    angles = positions.astype(jnp.float32)[..., None] * frequency
    cos_part, sin_part = jnp.cos(angles), jnp.sin(angles)
    return (
        jnp.concatenate([cos_part, cos_part], -1),
        jnp.concatenate([-sin_part, sin_part], -1),
    )


def rotated(rows, cos_part, sin_part):
    rows = rows.astype(jnp.float32)
    return (rows * cos_part + pltpu.roll(rows, HEAD_SIZE // 2, 1) * sin_part).astype(jnp.bfloat16)


def assemble_kernel(target_ref, table_ref, prefix_ref, kv_ref, cos_ref, sin_ref, *refs):
    chunks = range(len(CHUNKS))
    own, outs, (held, arrive, leave) = refs[0], refs[1:-3], refs[-3:]
    copies = [[] for _ in chunks]
    for c, count in enumerate(CHUNKS):
        for target in range(NBP // 4):
            for prompt in range(REQ_DEV):
                for b in range(count):
                    block = target * 4 + STARTS[c] + b
                    place = held.at[prompt, pl.ds(block * BLOCK_TOKENS, BLOCK_TOKENS)]
                    page = table_ref[prompt * NBP + block]
                    copies[c].append(
                        pltpu.make_async_copy(prefix_ref.at[page], place, arrive.at[c])
                    )
                    copies[c][-1].start()
    for prompt in range(REQ_DEV):
        rows = slice(prompt * STRETCH_TOKENS, (prompt + 1) * STRETCH_TOKENS)
        held[prompt, PRE:, :HEAD_SIZE] = rotated(
            kv_ref[rows, :HEAD_SIZE], cos_ref[...], sin_ref[...]
        )
        held[prompt, PRE:, HEAD_SIZE:] = kv_ref[rows, HEAD_SIZE:]
    out_copies = []
    for c, count in enumerate(CHUNKS):
        size = count * BLOCK_TOKENS
        for copy in copies[c]:
            copy.wait()
        for j in range(N_TP):
            first = (target_ref[j] * 4 + STARTS[c]) * BLOCK_TOKENS
            out_copies.append(
                pltpu.make_async_copy(
                    held.at[:, pl.ds(pl.multiple_of(first, BLOCK_TOKENS), size)],
                    outs[c * N_TP + j].at[:, pl.ds(0, size)],
                    leave.at[c],
                )
            )
            out_copies[-1].start()
    out_copies.append(pltpu.make_async_copy(held, own, leave.at[len(CHUNKS)]))
    out_copies[-1].start()
    for copy in out_copies:
        copy.wait()


def assembled(targets, table, prefix, kv, cos_part, sin_part):
    anywhere = pl.BlockSpec(memory_space=pltpu.HBM)
    whole = pl.BlockSpec(memory_space=pltpu.VMEM)
    scalars = pl.BlockSpec(memory_space=pltpu.SMEM)
    own = (REQ_DEV, PROMPT_BLOCKS * BLOCK_TOKENS, PAGE)
    shapes = [own] + [
        (REQ_DEV, travelling_rows(c), PAGE) for c in range(len(CHUNKS)) for _ in range(N_TP)
    ]
    outs = pl.pallas_call(
        assemble_kernel,
        in_specs=[scalars, scalars, anywhere, whole, whole, whole],
        out_specs=[anywhere] * len(shapes),
        out_shape=[jax.ShapeDtypeStruct(shape, jnp.bfloat16) for shape in shapes],
        scratch_shapes=[
            pltpu.VMEM(own, jnp.bfloat16),
            pltpu.SemaphoreType.DMA((len(CHUNKS),)),
            pltpu.SemaphoreType.DMA((len(CHUNKS) + 1,)),
        ],
        compiler_params=pltpu.CompilerParams(vmem_limit_bytes=VMEM),
        cost_estimate=LIGHT,
        name="assembled",
    )(targets, table, prefix, kv, cos_part, sin_part)
    return outs[0], [outs[1 + c * N_TP : 1 + (c + 1) * N_TP] for c in range(len(CHUNKS))]


def route_kernel(width, group_ref, prompt_ref, head_ref, *refs):
    arrived, (out, spread, packed, empty, sem) = refs[:N_TP], refs[N_TP:]
    prompt = pl.program_id(0)
    rows = width // HEADS

    @pl.when(prompt == 0)
    def _():
        empty[...] = jnp.zeros_like(empty)
        for d in range(N_REQ):

            @pl.when(prompt_ref[d] < 0)
            def _():
                pltpu.make_async_copy(empty, out.at[d], sem).start()

    for first in range(0, rows, BLOCK_TOKENS):
        size = min(BLOCK_TOKENS, rows - first)
        for half in range(2):
            lanes = pl.ds(half * HEAD_SIZE, HEAD_SIZE)
            for j in range(N_TP):
                places = pl.ds(first * HEADS + head_ref[j], size, stride=HEADS)
                block = arrived[j][0, pl.ds(first, max(size, RESULT_ROWS)), lanes]
                spread[half, places, :] = block.astype(jnp.float32)[:size]
            part = pl.ds(first * HEADS, size * HEADS)
            packed[prompt, part, lanes] = spread[half, part, :].astype(jnp.bfloat16)
    pltpu.make_async_copy(packed.at[prompt], out.at[group_ref[prompt]], sem).start()

    @pl.when(prompt == REQ_DEV - 1)
    def _():
        pltpu.make_async_copy(out, out, sem).wait()


def routed_pages(c, targets, prompts, heads, arrived):
    rows, width = travelling_rows(c), routed_rows(c)
    return pl.pallas_call(
        functools.partial(route_kernel, width),
        grid_spec=pltpu.PrefetchScalarGridSpec(
            num_scalar_prefetch=3,
            grid=(REQ_DEV,),
            in_specs=[pl.BlockSpec((1, rows, PAGE), lambda n, *_: (n, 0, 0))] * N_TP,
            out_specs=pl.BlockSpec(memory_space=pltpu.HBM),
            scratch_shapes=[
                pltpu.VMEM((2, width, HEAD_SIZE), jnp.float32),
                pltpu.VMEM((REQ_DEV, width, PAGE), jnp.bfloat16),
                pltpu.VMEM((width, PAGE), jnp.bfloat16),
                pltpu.SemaphoreType.DMA,
            ],
        ),
        out_shape=jax.ShapeDtypeStruct((N_REQ, width, PAGE), jnp.bfloat16),
        compiler_params=pltpu.CompilerParams(vmem_limit_bytes=VMEM),
        cost_estimate=LIGHT,
        name="routed_pages",
    )(targets, prompts, heads, *arrived)


def store_kernel(c, pieces, *refs):
    out, held, arrive, leave = refs[-4:]
    rows = CHUNKS[c] * BLOCK_TOKENS * HEADS
    place = pl.ds(STARTS[c] * BLOCK_TOKENS * HEADS, rows)
    ins, outs = [], []
    for slot in range(DECODE_SLOTS):
        source = pieces.at[other_side(slot), pl.ds(0, rows)]
        ins.append(pltpu.make_async_copy(source, held.at[slot], arrive.at[slot]))
        outs.append(pltpu.make_async_copy(held.at[slot], out.at[slot, place], leave.at[slot]))
    for copy in ins:
        copy.start()
    for slot in range(DECODE_SLOTS):
        ins[slot].wait()
        outs[slot].start()
    for copy in outs:
        copy.wait()


def stored_chunk(c, pieces, store):
    rows = CHUNKS[c] * BLOCK_TOKENS * HEADS
    operands = [pieces] + ([] if store is None else [store])
    anywhere = pl.BlockSpec(memory_space=pltpu.HBM)
    return pl.pallas_call(
        functools.partial(store_kernel, c),
        in_specs=[anywhere] * len(operands),
        out_specs=anywhere,
        out_shape=jax.ShapeDtypeStruct(
            (DECODE_SLOTS, 4 * BLOCK_TOKENS * HEADS, PAGE), jnp.bfloat16
        ),
        scratch_shapes=[
            pltpu.VMEM((DECODE_SLOTS, rows, PAGE), jnp.bfloat16),
            pltpu.SemaphoreType.DMA((DECODE_SLOTS,)),
            pltpu.SemaphoreType.DMA((DECODE_SLOTS,)),
        ],
        input_output_aliases={} if store is None else {1: 0},
        compiler_params=pltpu.CompilerParams(vmem_limit_bytes=VMEM),
        cost_estimate=LIGHT,
        name="stored_chunk",
    )(*operands)


def prefill_kernel(mask_ref, query_ref, cos_ref, sin_ref, *refs):
    page_ref = refs[0]
    out_ref, keys, values = refs[-3:]
    tokens = PROMPT_BLOCKS * BLOCK_TOKENS

    @pl.when(pl.program_id(0) == 0)
    def _():
        keys[:, :HEAD_SIZE] = page_ref[0, :, :HEAD_SIZE]
        values[:, :HEAD_SIZE] = page_ref[0, :, HEAD_SIZE:]
        block = lax.broadcasted_iota(jnp.int32, (tokens, HEAD_SIZE), 0) // BLOCK_TOKENS
        lane = lax.broadcasted_iota(jnp.int32, (tokens, HEAD_SIZE), 1)
        keys[:, HEAD_SIZE:] = jnp.where(block == lane, 1.0, 0.0).astype(jnp.bfloat16)
        values[:, HEAD_SIZE:] = jnp.ones((tokens, HEAD_SIZE), jnp.bfloat16)

    row = lax.broadcasted_iota(jnp.int32, (BLOCK_TOKENS, HEAD_SIZE), 0)
    column = lax.broadcasted_iota(jnp.int32, (BLOCK_TOKENS, HEAD_SIZE), 1)

    def masked_scores(head, first):
        lanes = slice(head * HEAD_SIZE, (head + 1) * HEAD_SIZE)
        rows = slice(first, first + QUERY_ROWS)
        blocks = range(first // BLOCK_TOKENS, (first + QUERY_ROWS) // BLOCK_TOKENS)
        width = PRE + -(-(first + QUERY_ROWS) // HEAD_SIZE) * HEAD_SIZE
        query = rotated(query_ref[rows, lanes], cos_ref[rows, :], sin_ref[rows, :])
        mask = jnp.concatenate(
            [
                jnp.broadcast_to(mask_ref[head, a : a + 1, :], (BLOCK_TOKENS, HEAD_SIZE))
                for a in blocks
            ],
            0,
        ).astype(jnp.bfloat16)
        scores = lax.dot_general(
            jnp.concatenate([query, mask], 1),
            keys[:width, :],
            (((1,), (1,)), ((), ())),
            preferred_element_type=jnp.float32,
        )
        parts = []
        for i, a in enumerate(blocks):
            part = scores[i * BLOCK_TOKENS : (i + 1) * BLOCK_TOKENS]
            start = PRE + a * BLOCK_TOKENS
            left = start // HEAD_SIZE * HEAD_SIZE
            right = left + HEAD_SIZE
            causal = column - (start - left) <= row
            pieces = [part[:, :left], jnp.where(causal, part[:, left:right], OFF)]
            if right < width:
                pieces.append(part[:, right:])
            parts.append(jnp.concatenate(pieces, 1))
        return jnp.concatenate(parts, 0)

    def attend(head, first, scores):
        peak = jnp.max(scores, axis=1, keepdims=True)
        weights = jnp.exp2((scores - peak) * EXP2_SCALE).astype(jnp.bfloat16)
        result = lax.dot_general(
            weights,
            values[: scores.shape[1], :],
            (((1,), (0,)), ((), ())),
            preferred_element_type=jnp.float32,
        )
        out_ref[first : first + QUERY_ROWS, head * HEAD_SIZE : (head + 1) * HEAD_SIZE] = (
            result[:, :HEAD_SIZE] / result[:, HEAD_SIZE:]
        ).astype(jnp.bfloat16)

    before = None
    for head in range(HEADS_AT_ONCE):
        for first in range(0, STRETCH_TOKENS, QUERY_ROWS):
            current = (head, first, masked_scores(head, first))
            if before is not None:
                attend(*before)
            before = current
    attend(*before)


def prefill_prompt(prompt, mask, query, cos_part, sin_part, pages, out):
    tables = pl.BlockSpec((STRETCH_TOKENS, HEAD_SIZE), lambda i: (0, 0))
    rows = pl.BlockSpec((STRETCH_TOKENS, HEADS_AT_ONCE * HEAD_SIZE), lambda i: (prompt, i))
    steps = HEADS // HEADS_AT_ONCE
    operands = [mask, query, cos_part, sin_part, pages] + ([] if out is None else [out])
    return pl.pallas_call(
        prefill_kernel,
        grid=(steps,),
        in_specs=[
            pl.BlockSpec(
                (HEADS_AT_ONCE, STRETCH_BLOCKS, HEAD_SIZE), lambda i: (prompt * steps + i, 0, 0)
            ),
            rows,
            tables,
            tables,
        ]
        + [pl.BlockSpec((1, PROMPT_BLOCKS * BLOCK_TOKENS, PAGE), lambda i: (prompt, 0, 0))]
        + ([] if out is None else [pl.BlockSpec(memory_space=pltpu.HBM)]),
        out_specs=rows,
        out_shape=jax.ShapeDtypeStruct(query.shape, query.dtype),
        scratch_shapes=[pltpu.VMEM((PROMPT_BLOCKS * BLOCK_TOKENS, PAGE), jnp.bfloat16)] * 2,
        input_output_aliases={} if out is None else {len(operands) - 1: 0},
        compiler_params=pltpu.CompilerParams(vmem_limit_bytes=VMEM),
        cost_estimate=LIGHT,
        name="prefill_prompt",
    )(*operands)


def decode_kernel(length_ref, query_ref, fresh_ref, cos_ref, sin_ref, picked_ref, *refs):
    page_ref, outs = refs[0], refs[-N_TP:]
    prompt = pl.program_id(0)
    lines = DECODE_STEPS * HEADS
    tokens = PROMPT_BLOCKS * BLOCK_TOKENS
    width = tokens + HEAD_SIZE

    def by_step(array, rows, step):
        return jnp.where(step == 0, array[0:1], array[1:2])

    line = lax.broadcasted_iota(jnp.int32, (lines, HEAD_SIZE), 0)
    line_step = line % HEADS // (HEADS // 2)
    query = rotated(
        query_ref[0],
        by_step(cos_ref[0], lines, line_step),
        by_step(sin_ref[0], lines, line_step),
    )
    place = lax.broadcasted_iota(jnp.int32, (HEAD_SIZE, HEAD_SIZE), 0)
    fresh = fresh_ref[0].astype(jnp.float32)
    cos_part, sin_part = (by_step(r[0], HEAD_SIZE, place) for r in (cos_ref, sin_ref))
    fresh_keys = by_step(fresh[:, :HEAD_SIZE], HEAD_SIZE, place)
    fresh_keys = rotated(jnp.where(place < DECODE_STEPS, fresh_keys, 0.0), cos_part, sin_part)
    fresh_values = by_step(fresh[:, HEAD_SIZE:], HEAD_SIZE, place)
    fresh_values = jnp.where(place < DECODE_STEPS, fresh_values, 0.0).astype(jnp.bfloat16)
    keys = jnp.concatenate([page_ref[0, :, :HEAD_SIZE], fresh_keys], 0)
    values = jnp.concatenate([page_ref[0, :, HEAD_SIZE:], fresh_values], 0)
    scores = lax.dot_general(
        query, keys, (((1,), (1,)), ((), ())), preferred_element_type=jnp.float32
    )
    number = lax.broadcasted_iota(jnp.int32, (lines, width), 1)
    block = number // BLOCK_TOKENS
    step = lax.broadcasted_iota(jnp.int32, (lines, width), 0) % HEADS // (HEADS // 2)
    picked = picked_ref[0]
    kept = block >= NBP
    for i in range(SELECTED_BLOCKS):
        kept = kept | (picked[:, i : i + 1] == block)
    kept = kept & (number < length_ref[prompt])
    kept = (kept & (number < tokens)) | ((number >= tokens) & (number - tokens <= step))
    scores = jnp.where(kept, scores, OFF)
    peak = jnp.max(scores, axis=1, keepdims=True)
    weights = jnp.where(kept, jnp.exp2((scores - peak) * EXP2_SCALE), 0.0)
    total = jnp.sum(weights, axis=1, keepdims=True)
    coarse = weights.astype(jnp.bfloat16)
    fine = (weights - coarse.astype(jnp.float32)).astype(jnp.bfloat16)
    result = lax.dot_general(
        jnp.concatenate([coarse, fine], 0),
        values,
        (((1,), (0,)), ((), ())),
        preferred_element_type=jnp.float32,
    )
    result = (result[:lines] + result[lines:]) / total
    result = jnp.concatenate([result[:HEADS], result[HEADS:]], 1)
    result = jnp.concatenate([result, jnp.zeros_like(result)], 0).astype(jnp.bfloat16)
    for out in outs:
        out[0] = result


def decoded(lengths, query, fresh, cos_part, sin_part, picked, pages, leaving):
    def one(array):
        return pl.BlockSpec((1,) + array.shape[1:], lambda n, *_: (n, 0, 0))

    operands = [query, fresh, cos_part, sin_part, picked, pages]
    place = CHUNKS[-1] * BLOCK_TOKENS // RESULT_ROWS
    return pl.pallas_call(
        decode_kernel,
        grid_spec=pltpu.PrefetchScalarGridSpec(
            num_scalar_prefetch=1,
            grid=(REQ_DEV,),
            in_specs=[one(x) for x in operands] + [pl.BlockSpec(memory_space=pltpu.HBM)] * N_TP,
            out_specs=[pl.BlockSpec((1, RESULT_ROWS, PAGE), lambda n, *_: (n, place, 0))] * N_TP,
        ),
        out_shape=[jax.ShapeDtypeStruct(x.shape, jnp.bfloat16) for x in leaving],
        input_output_aliases={1 + len(operands) + j: j for j in range(N_TP)},
        compiler_params=pltpu.CompilerParams(vmem_limit_bytes=VMEM),
        cost_estimate=LIGHT,
        name="decoded",
    )(lengths, *operands, *leaving)


def after(array, *others):
    return lax.optimization_barrier((array, *others))[0]


def shards(
    stretch_query,
    stretch_kv,
    prefix_page_store,
    page_table,
    vs_mask,
    prompt_lengths,
    placement,
    step_query_rows,
    step_key_value,
    selected_prefix_blocks,
):
    axes = ("section", "req", "tp")
    section = lax.axis_index("section")
    req = lax.axis_index("req")
    tp = lax.axis_index("tp")
    last = len(CHUNKS) - 1

    def across(leaving):
        return [
            lax.ppermute(pages, axes, cross_route(offset))
            for pages, offset in zip(leaving, TP_OFFSETS)
        ]

    cos_part, sin_part = rope_tables(PRE + jnp.arange(STRETCH_TOKENS, dtype=jnp.int32))
    tp_targets = jnp.stack([tp_moved(tp, offset) for offset in TP_OFFSETS]).astype(jnp.int32)
    pages, leaving = assembled(
        tp_targets,
        page_table.reshape(-1),
        prefix_page_store.reshape(PREFIX_PAGES, BLOCK_TOKENS, PAGE),
        stretch_kv.reshape(-1, PAGE),
        cos_part,
        sin_part,
    )
    arrived = [across(chunk) for chunk in leaving[:last]]

    own_heads = HEADS * HEAD_SIZE
    queries = lax.dynamic_slice_in_dim(after(step_query_rows, pages)[0], tp * own_heads, own_heads, 2)
    fresh = lax.dynamic_index_in_dim(step_key_value[0], tp, 2, keepdims=False)
    picks = lax.dynamic_slice_in_dim(selected_prefix_blocks[0], tp * HEADS, HEADS, 2)
    load = jnp.concatenate(
        [queries, fresh, picks.astype(jnp.bfloat16).reshape(DECODE_SLOTS, DECODE_STEPS, -1)],
        axis=-1,
    )
    sections = jnp.arange(2, dtype=jnp.int32)[:, None, None, None]
    load = jnp.where(sections == 1 - section, load[None], jnp.zeros((), load.dtype))
    load = lax.all_to_all(
        load.reshape((2 * N_REQ,) + load.shape[2:]),
        ("section", "req"),
        split_axis=0,
        concat_axis=0,
        tiled=True,
    )

    mask = jnp.where(vs_mask == 1, 0.0, OFF).reshape(-1, STRETCH_BLOCKS, PROMPT_BLOCKS)
    mask = jnp.pad(mask, ((0, 0), (0, 0), (0, HEAD_SIZE - PROMPT_BLOCKS)))

    def prefilled(prompt, out, *others):
        return prefill_prompt(
            prompt, after(mask, *others), stretch_query, cos_part, sin_part, pages, out
        )

    own_row = section * N_REQ + req
    targets = lax.dynamic_index_in_dim(placement, own_row, 0, keepdims=False)
    load = jnp.take(load, (1 - section) * N_REQ + targets, axis=0)
    lengths = PRE + lax.dynamic_slice_in_dim(prompt_lengths, own_row * REQ_DEV, REQ_DEV, 0)
    steps = jnp.arange(DECODE_STEPS, dtype=jnp.int32)
    step_cos, step_sin = rope_tables(lengths[:, None] + steps)

    def by_line(array):
        array = array.reshape(REQ_DEV, DECODE_STEPS, HEADS // 2, 2, -1)
        return jnp.transpose(array, (0, 3, 1, 2, 4)).reshape(REQ_DEV, DECODE_STEPS * HEADS, -1)

    origin = (1 - section) * N_REQ + other_side(req)
    origin_targets = lax.dynamic_index_in_dim(placement, origin, 0, keepdims=False)
    number = jnp.arange(REQ_DEV, dtype=jnp.int32)
    group = jnp.arange(N_REQ, dtype=jnp.int32)
    prompts = jnp.max(jnp.where(origin_targets == group[:, None], number, -1), axis=-1)

    def over_req(pages):
        return lax.all_to_all(pages, "req", split_axis=0, concat_axis=0, tiled=True)

    heads = jnp.stack([tp_moved(tp, offset, -1) for offset in TP_OFFSETS]).astype(jnp.int32)
    prefill_out = None
    waiting = []
    store = None
    before = None
    for step in ORDER:
        step, _, piece = step.partition("@")
        kind, n = step[0], int(step[1:] or 0)
        others = () if before is None else (before,)
        if piece:
            others += (arrived[int(piece[0])][int(piece[1])],)
        if kind == "d":
            full_last = decoded(
                after(lengths, *others),
                by_line(load[..., :own_heads]),
                load[..., own_heads : own_heads + PAGE],
                step_cos,
                step_sin,
                by_line(load[..., own_heads + PAGE :]).astype(jnp.int32),
                pages,
                leaving[last],
            )
            arrived.append(across(full_last))
            before = full_last[0]
        elif kind == "r":
            chunk = list(arrived[n])
            chunk[0] = after(chunk[0], *others)
            before = routed_pages(n, origin_targets, prompts, heads, chunk)
            waiting.append(over_req(before))
        elif kind == "p":
            before = prefill_out = prefilled(n, prefill_out, *others)
        else:
            before = store = stored_chunk(n, after(waiting[n], *others), store)
    routed = waiting[last]
    store = store.reshape(1, DECODE_SLOTS, 4, BLOCK_TOKENS, KEY_VALUE_HEADS, PAGE)
    first = CHUNKS[last] * BLOCK_TOKENS * HEADS
    results = routed[:, first : first + HEADS * KEY_VALUE_HEADS]
    results = results.reshape(2, N_REQ // 2, DECODE_STEPS, HEADS // 2, KEY_VALUE_HEADS, PAGE)
    results = jnp.transpose(results[::-1], (0, 1, 2, 4, 3, 5))
    decode_output = results.reshape(1, DECODE_SLOTS, DECODE_STEPS, QUERY_HEADS * HEAD_SIZE)
    return (prefill_out, store, decode_output)


def solution(mesh):
    placed = (
        P(("section", "req"), "tp"),
        P(("section", "req"), "tp", None),
        P(("section", "req"), None, "tp", None),
        P(("section", "req"), None),
        P(("section", "req"), "tp", None, None),
        P(),
        P(),
        P(("section", "req"), None, None, None),
        P(("section", "req"), None, None, None, None),
        P(("section", "req"), None, None, None, None),
    )
    return jax.shard_map(
        shards,
        mesh=mesh,
        in_specs=placed,
        out_specs=(
            P(("section", "req"), "tp"),
            P(("section", "req"), None, "tp", None, None, None),
            P(("section", "req"), None, None, None),
        ),
        check_vma=False,
    )
```

time: 946 us -> 209 us (0.22); the launches traced: 933 us -> 207 us
  blocking collectives: 250 us -> 0 us
  local copies, waits for them, and re-layouts: 196 us -> 10.6 us
  waiting for transfers between devices: 207 us -> 45 us
  other arithmetic: 136 us -> 4.83 us
  matrix products: 115 us -> 0 us
  Pallas kernels: 0 us -> 80.2 us
  starting transfers between devices: 3.31 us -> 64.7 us
  between operations: 14.7 us -> 1.3 us
  loops' own time: 11.3 us -> 0 us
    all_to_all x2 -> x0, blocking collectives: 201 us -> none  [the longest x1 101 us: shards(): lax.all_to_all(lax.all_to_all(route_buffer(prompt_page_list, targets, gro...]
    ppermute x1 -> x16, waiting for transfers between devices: 173 us -> 9.61 us  [across(): lax.ppermute(pages, axes, cross_route(offset))]
    dot_general x13 -> x0, matrix products: 115 us -> none  [the longest x4 51 us: prefill_request(): jnp.einsum('hqid,hqtd->hqit', query_blocks, key_tiles[..., :HEAD_SIZE], p...]
    gather x22 -> x1, local copies, waits for them, and re-layouts: 113 us -> 0.6 us  [shards(): load = jnp.take(load, (1 - section) * N_REQ + targets, axis=0)]
    pallas_call x0 -> x10, Pallas kernels: none -> 80.2 us  [the longest x4 50.2 us: prefill_prompt(): pl.pallas_call(prefill_kernel, grid=(steps,), in_specs=[pl.BlockSpec((HEA...]
    sub x8 -> x0, other arithmetic: 74.3 us -> none  [the longest x4 74.3 us: prefill_request(): weights = jnp.where(active_flag, jnp.exp(scores - row_peak), 0.0)]
    ppermute x1 -> x16, starting transfers between devices: 3.28 us -> 48 us  [across(): lax.ppermute(pages, axes, cross_route(offset))]
    all_to_all x0 -> x3, waiting for transfers between devices: none -> 35.4 us  [the longest x2 35.4 us: over_req(): return lax.all_to_all(pages, 'req', split_axis=0, concat_axis=0, tiled=True)]
  transfers between devices with their start and end apart: 2 -> 19, of which waited for: 2 -> 6; matrix products, arithmetic and copies ran while one was open for 1% -> 3% of each run, Pallas kernels for 0% -> 32%
where the time goes in v1:
time: 209 us; the launch traced here: 207 us
  Pallas kernels  80.2 us (38%)
  starting transfers between devices  64.7 us (31%)
  waiting for transfers between devices  45 us (22%)
  local copies, waits for them, and re-layouts  10.6 us (5%)
  other arithmetic  4.83 us (2%)
    pallas_call x4, Pallas kernels, prefill_prompt(): pl.pallas_call(prefill_kernel, grid=(steps,), in_specs=[pl.BlockSpec((HEA...  50.2 us
    ppermute x16, starting transfers between devices, across(): lax.ppermute(pages, axes, cross_route(offset))  48 us
    all_to_all x2, waiting for transfers between devices, over_req(): return lax.all_to_all(pages, 'req', split_axis=0, concat_axis=0, tiled=True)  35.4 us
    pallas_call x2, Pallas kernels, routed_pages(): pl.pallas_call(functools.partial(route_kernel, width), grid_spec=pltpu.Pr...  10.9 us
    ppermute x16, waiting for transfers between devices, across(): lax.ppermute(pages, axes, cross_route(offset))  9.61 us
    all_to_all x2, starting transfers between devices, over_req(): return lax.all_to_all(pages, 'req', split_axis=0, concat_axis=0, tiled=True)  9.57 us
    pallas_call x2, Pallas kernels, stored_chunk(): pl.pallas_call(functools.partial(store_kernel, c), in_specs=[anywhere] *...  7.15 us
    all_to_all x1, starting transfers between devices, shards(): lax.all_to_all(load.reshape((2 * N_REQ,) + load.shape[2:]), ('section', '...  7.12 us
  transfers between devices with their start and end apart: 19, of which 6 were waited for; matrix products, arithmetic and copies ran while one was open for 3% of the time, Pallas kernels for 32%

profile of v1, /device:TPU:0, one launch (start us, length us, event | category | flops | bytes accessed | tf_op | source)
XLA Modules:
  0.0 206.7 jit_solution(2302261927236585938)
XLA Ops:
  0.8 1.3 reshape.122.table_ref
  3.1 1.0 pad_maximum_fusion
  4.8 6.1 %assembled.1 = (bf16[4,2048,256]{2,1,0:T(8,128)(2,1)}, bf16[4,128,256]{2,1,0:T(8,128)(2,1)}, bf16[4,128,256]{2,1,0:T(8,128)(2,1)}, bf16[4,128,256]{2,1,0:T(8,128...) custom-call(s32[8]{0:T(128)} %stack.65.target_ref, ...), custom_call_target="tpu_custom_call" | custom-call | flops 1 | bytes 1 | tf_op jit(solution)/shard_map/assembled/pallas_call | solution.py:149
  13.2 7.1 %all-to-all-start = ((bf16[16,2,1344]{2,1,0:T(2,128)(2,1)}), bf16[16,2,1344]{2,1,0:T(2,128)(2,1)S(1)}, u32[]{:S(2)}, u32[]{:S(2)}) async-start(bf16[16,2,1344]{2,1,0:T(2,128)(2,1)} %broadcast_select_fusion), calls=%async_computation | async-start | bytes 180224 | tf_op jit(solution)/shard_map/all_to_all | solution.py:490
  20.3 3.1 %collective-permute-start = (bf16[4,128,256]{2,1,0:T(8,128)(2,1)}, bf16[4,128,256]{2,1,0:T(8,128)(2,1)S(1)}, u32[]{:S(2)}, u32[]{:S(2)}) collective-permute-start(bf16[4,128,256]{2,1,0:T(8,128)(2,1)} %get-tuple-element.38), channel_id=1, source_target_pairs={{0,96},{1,97},{2,98},{3,99},{4,100},{5,101},{6,102},{7,103},{8,104... | collective-permute-start | bytes 786440 | tf_op jit(solution)/shard_map/ppermute | solution.py:464
  23.4 3.5 %collective-permute-start.2 = (bf16[4,128,256]{2,1,0:T(8,128)(2,1)}, bf16[4,128,256]{2,1,0:T(8,128)(2,1)S(1)}, u32[]{:S(2)}, u32[]{:S(2)}) collective-permute-start(bf16[4,128,256]{2,1,0:T(8,128)(2,1)} %get-tuple-element.51), channel_id=1, source_target_pairs={{0,100},{1,101},{2,102},{3,103},{4,96},{5,97},{6,98},{7,99},{8,108... | collective-permute-start | bytes 786440 | tf_op jit(solution)/shard_map/ppermute | solution.py:464
  26.9 1.4 collective-permute-start.3
  28.3 2.1 %collective-permute-start.4 = (bf16[4,128,256]{2,1,0:T(8,128)(2,1)}, bf16[4,128,256]{2,1,0:T(8,128)(2,1)S(1)}, u32[]{:S(2)}, u32[]{:S(2)}) collective-permute-start(bf16[4,128,256]{2,1,0:T(8,128)(2,1)} %get-tuple-element.55), channel_id=1, source_target_pairs={{0,98},{1,99},{2,100},{3,101},{4,102},{5,103},{6,96},{7,97},{8,106... | collective-permute-start | bytes 786440 | tf_op jit(solution)/shard_map/ppermute | solution.py:464
  35.0 4.9 %collective-permute-start.6 = (bf16[4,128,256]{2,1,0:T(8,128)(2,1)}, bf16[4,128,256]{2,1,0:T(8,128)(2,1)S(1)}, u32[]{:S(2)}, u32[]{:S(2)}) collective-permute-start(bf16[4,128,256]{2,1,0:T(8,128)(2,1)} %get-tuple-element.57), channel_id=1, source_target_pairs={{0,101},{1,100},{2,103},{3,102},{4,97},{5,96},{6,99},{7,98},{8,109... | collective-permute-start | bytes 786440 | tf_op jit(solution)/shard_map/ppermute | solution.py:464
  40.5 2.7 %collective-permute-start.7 = (bf16[4,128,256]{2,1,0:T(8,128)(2,1)}, bf16[4,128,256]{2,1,0:T(8,128)(2,1)S(1)}, u32[]{:S(2)}, u32[]{:S(2)}) collective-permute-start(bf16[4,128,256]{2,1,0:T(8,128)(2,1)} %get-tuple-element.58), channel_id=1, source_target_pairs={{0,102},{1,103},{2,96},{3,97},{4,98},{5,99},{6,100},{7,101},{8,110... | collective-permute-start | bytes 786440 | tf_op jit(solution)/shard_map/ppermute | solution.py:464
  43.2 5.3 %collective-permute-start.8 = (bf16[4,128,256]{2,1,0:T(8,128)(2,1)}, bf16[4,128,256]{2,1,0:T(8,128)(2,1)S(1)}, u32[]{:S(2)}, u32[]{:S(2)}) collective-permute-start(bf16[4,128,256]{2,1,0:T(8,128)(2,1)} %get-tuple-element.59), channel_id=1, source_target_pairs={{0,103},{1,102},{2,97},{3,96},{4,99},{5,98},{6,101},{7,100},{8,111... | collective-permute-start | bytes 786440 | tf_op jit(solution)/shard_map/ppermute | solution.py:464
  50.6 5.9 %decoded.1 = (bf16[4,144,256]{2,1,0:T(8,128)(2,1)}, bf16[4,144,256]{2,1,0:T(8,128)(2,1)}, bf16[4,144,256]{2,1,0:T(8,128)(2,1)}, bf16[4,144,256]{2,1,0:T(8,128)(2...) custom-call(s32[4]{0:T(128)} %copy-done.28, ...), custom_call_target="tpu_custom_call", output_to_operand_aliasing={{0}: (7, {}), {1}: (8, {}), {2}: (9, {}), {3}: (10, {}), {4... | custom-call | flops 1 | bytes 1 | tf_op jit(solution)/shard_map/decoded/pallas_call | solution.py:424
  56.5 12.6 %prefill_prompt.4.refs_1_ = bf16[2048,1024]{1,0:T(8,128)(2,1)} custom-call(f32[32,8,128]{2,1,0:T(8,128)} %pad.4.mask_ref, bf16[2048,1024]{1,0:T(8,128)(2,1)} %query_ref.7, f32[512,128]{1,0:T(8,128)} %get-tuple-element.81.cos_ref, f32[512,128]{1,0:T(8,128)} %get-tuple-element.82.sin_ref, bf16[4,2048,256]{2,1,0:T(8,128)(2,1)} %get-tuple-element.40.refs_0_), custom_call_target="tpu_custom_call" | custom-call | flops 1 | bytes 1 | tf_op jit(solution)/shard_map/prefill_prompt/pallas_call | solution.py:338
  70.8 5.3 %routed_pages.2 = bf16[8,1024,256]{2,1,0:T(8,128)(2,1)} custom-call(s32[4]{0:T(128)} %copy-done.27, s32[8]{0:T(128)} %select_reduce_fusion.prompt_ref, s32[8]{0:T(128)} %stack.58.head_ref, bf16[4,128,256]{2,1,0:T(8,128)(2,1)} %copy-done.16, bf16[4,128,256]{2,1,0:T(8,128)(2,1)} %copy-done.18, bf16[4,128,256]{2,1,0:T(8,128)(2,1)} %copy-done.19, ...), custom_call_target="tpu_custom_call" | custom-call | flops 1 | bytes 1 | tf_op jit(solution)/shard_map/routed_pages/pallas_call | solution.py:199
  76.1 4.7 %all-to-all-start.2 = ((bf16[8,1024,256]{2,1,0:T(8,128)(2,1)}), bf16[8,1024,256]{2,1,0:T(8,128)(2,1)}, u32[]{:S(2)}, u32[]{:S(2)}) async-start(bf16[8,1024,256]{2,1,0:T(8,128)(2,1)} %routed_pages.2), calls=%async_computation.2 | async-start | bytes 8388608 | tf_op jit(solution)/shard_map/all_to_all | solution.py:524
  80.9 2.8 %collective-permute-start.1 = (bf16[4,144,256]{2,1,0:T(8,128)(2,1)S(1)}, bf16[4,144,256]{2,1,0:T(8,128)(2,1)S(1)}, u32[]{:S(2)}, u32[]{:S(2)}) collective-permute-start(bf16[4,144,256]{2,1,0:T(8,128)(2,1)S(1)} %copy-done.1), channel_id=1, source_target_pairs={{0,96},{1,97},{2,98},{3,99},{4,100},{5,101},{6,102},{7,103},{8,104... | collective-permute-start | bytes 884744 | tf_op jit(solution)/shard_map/ppermute | solution.py:464
  83.6 3.0 %collective-permute-start.9 = (bf16[4,144,256]{2,1,0:T(8,128)(2,1)S(1)}, bf16[4,144,256]{2,1,0:T(8,128)(2,1)S(1)}, u32[]{:S(2)}, u32[]{:S(2)}) collective-permute-start(bf16[4,144,256]{2,1,0:T(8,128)(2,1)S(1)} %copy-done.4), channel_id=1, source_target_pairs={{0,99},{1,98},{2,101},{3,100},{4,103},{5,102},{6,97},{7,96},{8,107... | collective-permute-start | bytes 884744 | tf_op jit(solution)/shard_map/ppermute | solution.py:464
  86.7 2.2 %collective-permute-start.10 = (bf16[4,144,256]{2,1,0:T(8,128)(2,1)S(1)}, bf16[4,144,256]{2,1,0:T(8,128)(2,1)S(1)}, u32[]{:S(2)}, u32[]{:S(2)}) collective-permute-start(bf16[4,144,256]{2,1,0:T(8,128)(2,1)S(1)} %copy-done.2), channel_id=1, source_target_pairs={{0,97},{1,96},{2,99},{3,98},{4,101},{5,100},{6,103},{7,102},{8,105... | collective-permute-start | bytes 884744 | tf_op jit(solution)/shard_map/ppermute | solution.py:464
  89.4 3.4 %collective-permute-start.12 = (bf16[4,144,256]{2,1,0:T(8,128)(2,1)S(1)}, bf16[4,144,256]{2,1,0:T(8,128)(2,1)}, u32[]{:S(2)}, u32[]{:S(2)}) collective-permute-start(bf16[4,144,256]{2,1,0:T(8,128)(2,1)S(1)} %copy-done.5), channel_id=1, source_target_pairs={{0,100},{1,101},{2,102},{3,103},{4,96},{5,97},{6,98},{7,99},{8,108... | collective-permute-start | bytes 884744 | tf_op jit(solution)/shard_map/ppermute | solution.py:464
  92.9 4.4 %collective-permute-start.13 = (bf16[4,144,256]{2,1,0:T(8,128)(2,1)S(1)}, bf16[4,144,256]{2,1,0:T(8,128)(2,1)S(1)}, u32[]{:S(2)}, u32[]{:S(2)}) collective-permute-start(bf16[4,144,256]{2,1,0:T(8,128)(2,1)S(1)} %copy-done.6), channel_id=1, source_target_pairs={{0,101},{1,100},{2,103},{3,102},{4,97},{5,96},{6,99},{7,98},{8,109... | collective-permute-start | bytes 884744 | tf_op jit(solution)/shard_map/ppermute | solution.py:464
  97.2 3.0 %collective-permute-done.9.refs_3_ = bf16[4,144,256]{2,1,0:T(8,128)(2,1)S(1)} collective-permute-done((bf16[4,144,256]{2,1,0:T(8,128)(2,1)S(1)}, bf16[4,144,256]{2,1,0:T(8,128)(2,1)S(1)}, u32[]{:S(2)}, u32[]{:S(2)}) %collective-permute-start.9) | collective-permute-done | bytes 294944 | tf_op jit(solution)/shard_map/ppermute | solution.py:464
  100.3 3.5 %collective-permute-start.14 = (bf16[4,144,256]{2,1,0:T(8,128)(2,1)S(1)}, bf16[4,144,256]{2,1,0:T(8,128)(2,1)S(1)}, u32[]{:S(2)}, u32[]{:S(2)}) collective-permute-start(bf16[4,144,256]{2,1,0:T(8,128)(2,1)S(1)} %copy-done.7), channel_id=1, source_target_pairs={{0,102},{1,103},{2,96},{3,97},{4,98},{5,99},{6,100},{7,101},{8,110... | collective-permute-start | bytes 884744 | tf_op jit(solution)/shard_map/ppermute | solution.py:464
  104.7 4.4 %collective-permute-start.15 = (bf16[4,144,256]{2,1,0:T(8,128)(2,1)S(1)}, bf16[4,144,256]{2,1,0:T(8,128)(2,1)S(1)}, u32[]{:S(2)}, u32[]{:S(2)}) collective-permute-start(bf16[4,144,256]{2,1,0:T(8,128)(2,1)S(1)} %copy-done.8), channel_id=1, source_target_pairs={{0,103},{1,102},{2,97},{3,96},{4,99},{5,98},{6,101},{7,100},{8,111... | collective-permute-start | bytes 884744 | tf_op jit(solution)/shard_map/ppermute | solution.py:464
  109.2 12.5 %prefill_prompt.5.refs_1_ = bf16[2048,1024]{1,0:T(8,128)(2,1)} custom-call(f32[32,8,128]{2,1,0:T(8,128)} %pad.4.mask_ref, bf16[2048,1024]{1,0:T(8,128)(2,1)} %query_ref.7, f32[512,128]{1,0:T(8,128)} %get-tuple-element.81.cos_ref, f32[512,128]{1,0:T(8,128)} %get-tuple-element.82.sin_ref, ...), custom_call_target="tpu_custom_call", output_to_operand_aliasing={{}: (5, {})} | custom-call | flops 1 | bytes 1 | tf_op jit(solution)/shard_map/prefill_prompt/pallas_call | solution.py:338
  121.7 12.5 %prefill_prompt.6.refs_1_ = bf16[2048,1024]{1,0:T(8,128)(2,1)} custom-call(f32[32,8,128]{2,1,0:T(8,128)} %pad.4.mask_ref, bf16[2048,1024]{1,0:T(8,128)(2,1)} %query_ref.7, f32[512,128]{1,0:T(8,128)} %get-tuple-element.81.cos_ref, f32[512,128]{1,0:T(8,128)} %get-tuple-element.82.sin_ref, ...), custom_call_target="tpu_custom_call", output_to_operand_aliasing={{}: (5, {})} | custom-call | flops 1 | bytes 1 | tf_op jit(solution)/shard_map/prefill_prompt/pallas_call | solution.py:338
  134.3 4.1 %collective-permute-done.15.refs_7_ = bf16[4,144,256]{2,1,0:T(8,128)(2,1)S(1)} collective-permute-done((bf16[4,144,256]{2,1,0:T(8,128)(2,1)S(1)}, bf16[4,144,256]{2,1,0:T(8,128)(2,1)S(1)}, u32[]{:S(2)}, u32[]{:S(2)}) %collective-permute-start.15) | collective-permute-done | bytes 294944 | tf_op jit(solution)/shard_map/ppermute | solution.py:464
  139.1 5.6 %routed_pages.3 = bf16[8,1088,256]{2,1,0:T(8,128)(2,1)} custom-call(s32[4]{0:T(128)} %copy-done.27, s32[8]{0:T(128)} %select_reduce_fusion.prompt_ref, s32[8]{0:T(128)} %stack.58.head_ref, bf16[4,144,256]{2,1,0:T(8,128)(2,1)} %copy-done.9, bf16[4,144,256]{2,1,0:T(8,128)(2,1)} %copy-done.11, bf16[4,144,256]{2,1,0:T(8,128)(2,1)} %copy-done.12, ...), custom_call_target="tpu_custom_call" | custom-call | flops 1 | bytes 1 | tf_op jit(solution)/shard_map/routed_pages/pallas_call | solution.py:199
  144.7 4.9 %all-to-all-start.1 = ((bf16[8,1088,256]{2,1,0:T(8,128)(2,1)}), bf16[8,1088,256]{2,1,0:T(8,128)(2,1)}, u32[]{:S(2)}, u32[]{:S(2)}) async-start(bf16[8,1088,256]{2,1,0:T(8,128)(2,1)} %routed_pages.3), calls=%async_computation.1 | async-start | bytes 8912896 | tf_op jit(solution)/shard_map/all_to_all | solution.py:524
  149.6 12.5 %prefill_prompt.7 = bf16[2048,1024]{1,0:T(8,128)(2,1)} custom-call(f32[32,8,128]{2,1,0:T(8,128)} %pad.4.mask_ref, bf16[2048,1024]{1,0:T(8,128)(2,1)} %query_ref.7, f32[512,128]{1,0:T(8,128)} %get-tuple-element.81.cos_ref, f32[512,128]{1,0:T(8,128)} %get-tuple-element.82.sin_ref, ...), custom_call_target="tpu_custom_call", output_to_operand_aliasing={{}: (5, {})} | custom-call | flops 1 | bytes 1 | tf_op jit(solution)/shard_map/prefill_prompt/pallas_call | solution.py:338
  162.2 3.6 %stored_chunk.2.refs_0_ = bf16[8,2048,256]{2,1,0:T(8,128)(2,1)} custom-call(bf16[8,1024,256]{2,1,0:T(8,128)(2,1)} %all-to-all-done.2.pieces), custom_call_target="tpu_custom_call" | custom-call | flops 1 | bytes 1 | tf_op jit(solution)/shard_map/stored_chunk/pallas_call | solution.py:242
  165.7 35.4 %all-to-all-done.1.pieces = bf16[8,1088,256]{2,1,0:T(8,128)(2,1)} async-done(((bf16[8,1088,256]{2,1,0:T(8,128)(2,1)}), bf16[8,1088,256]{2,1,0:T(8,128)(2,1)}, u32[]{:S(2)}, u32[]{:S(2)}) %all-to-all-start.1) | async-done | bytes 4456480 | tf_op jit(solution)/shard_map/all_to_all | solution.py:524
  201.2 3.6 %stored_chunk.3 = bf16[8,2048,256]{2,1,0:T(8,128)(2,1)} custom-call(bf16[8,1088,256]{2,1,0:T(8,128)(2,1)} %all-to-all-done.1.pieces, bf16[8,2048,256]{2,1,0:T(8,128)(2,1)} %stored_chunk.2.refs_0_), custom_call_target="tpu_custom_call", output_to_operand_aliasing={{}: (1, {})} | custom-call | flops 1 | bytes 1 | tf_op jit(solution)/shard_map/stored_chunk/pallas_call | solution.py:242
  (119 shorter events, 16.9 us)
Async XLA Ops:
  0.7 30.5 %copy-start.26 = (s32[16,4]{0,1:T(4,128)S(1)}, s32[16,4]{0,1:T(4,128)}, u32[]{:S(2)}) copy-start(s32[16,4]{0,1:T(4,128)} %param.16) | copy-start | bytes 772
  0.7 30.7 %copy-start.29 = (s32[64]{0:T(128)S(1)}, s32[64]{0:T(128)}, u32[]{:S(2)}) copy-start(s32[64]{0:T(128)} %param.15) | copy-start | bytes 772
  0.7 31.0 %copy-start.24 = (s32[4,8,8,32]{3,2,1,0:T(8,128)S(1)}, s32[4,8,8,32]{3,2,1,0:T(8,128)}, u32[]{:S(2)}) copy-start(s32[4,8,8,32]{3,2,1,0:T(8,128)} %param.14) | copy-start | bytes 98308
  13.2 21.2 %all-to-all-start = ((bf16[16,2,1344]{2,1,0:T(2,128)(2,1)}), bf16[16,2,1344]{2,1,0:T(2,128)(2,1)S(1)}, u32[]{:S(2)}, u32[]{:S(2)}) async-start(bf16[16,2,1344]{2,1,0:T(2,128)(2,1)} %broadcast_select_fusion), calls=%async_computation | async-start | bytes 180224 | tf_op jit(solution)/shard_map/all_to_all | solution.py:490
  20.3 14.7 %collective-permute-start = (bf16[4,128,256]{2,1,0:T(8,128)(2,1)}, bf16[4,128,256]{2,1,0:T(8,128)(2,1)S(1)}, u32[]{:S(2)}, u32[]{:S(2)}) collective-permute-start(bf16[4,128,256]{2,1,0:T(8,128)(2,1)} %get-tuple-element.38), channel_id=1, source_target_pairs={{0,96},{1,97},{2,98},{3,99},{4,100},{5,101},{6,102},{7,103},{8,104... | collective-permute-start | bytes 786440 | tf_op jit(solution)/shard_map/ppermute | solution.py:464
  23.4 17.1 %collective-permute-start.2 = (bf16[4,128,256]{2,1,0:T(8,128)(2,1)}, bf16[4,128,256]{2,1,0:T(8,128)(2,1)S(1)}, u32[]{:S(2)}, u32[]{:S(2)}) collective-permute-start(bf16[4,128,256]{2,1,0:T(8,128)(2,1)} %get-tuple-element.51), channel_id=1, source_target_pairs={{0,100},{1,101},{2,102},{3,103},{4,96},{5,97},{6,98},{7,99},{8,108... | collective-permute-start | bytes 786440 | tf_op jit(solution)/shard_map/ppermute | solution.py:464
  26.9 16.3 %collective-permute-start.3 = (bf16[4,128,256]{2,1,0:T(8,128)(2,1)}, bf16[4,128,256]{2,1,0:T(8,128)(2,1)S(1)}, u32[]{:S(2)}, u32[]{:S(2)}) collective-permute-start(bf16[4,128,256]{2,1,0:T(8,128)(2,1)} %get-tuple-element.54), channel_id=1, source_target_pairs={{0,97},{1,96},{2,99},{3,98},{4,101},{5,100},{6,103},{7,102},{8,105... | collective-permute-start | bytes 786440 | tf_op jit(solution)/shard_map/ppermute | solution.py:464
  28.3 40.8 %collective-permute-start.4 = (bf16[4,128,256]{2,1,0:T(8,128)(2,1)}, bf16[4,128,256]{2,1,0:T(8,128)(2,1)S(1)}, u32[]{:S(2)}, u32[]{:S(2)}) collective-permute-start(bf16[4,128,256]{2,1,0:T(8,128)(2,1)} %get-tuple-element.55), channel_id=1, source_target_pairs={{0,98},{1,99},{2,100},{3,101},{4,102},{5,103},{6,96},{7,97},{8,106... | collective-permute-start | bytes 786440 | tf_op jit(solution)/shard_map/ppermute | solution.py:464
  30.4 38.7 %collective-permute-start.5 = (bf16[4,128,256]{2,1,0:T(8,128)(2,1)}, bf16[4,128,256]{2,1,0:T(8,128)(2,1)S(1)}, u32[]{:S(2)}, u32[]{:S(2)}) collective-permute-start(bf16[4,128,256]{2,1,0:T(8,128)(2,1)} %get-tuple-element.56), channel_id=1, source_target_pairs={{0,99},{1,98},{2,101},{3,100},{4,103},{5,102},{6,97},{7,96},{8,107... | collective-permute-start | bytes 786440 | tf_op jit(solution)/shard_map/ppermute | solution.py:464
  31.3 37.7 %copy-start.27 = (s32[4]{0:T(128)}, s32[4]{0:T(128)S(1)}, u32[]{:S(2)}) copy-start(s32[4]{0:T(128)S(1)} %get-tuple-element.74.group_ref) | copy-start | bytes 52
  31.5 19.1 %copy-start.28 = (s32[4]{0:T(128)}, s32[4]{0:T(128)S(1)}, u32[]{:S(2)}) copy-start(s32[4]{0:T(128)S(1)} %dynamic-slice_add_fusion.length_ref) | copy-start | bytes 52
  35.0 34.1 %copy-start.16 = (bf16[4,128,256]{2,1,0:T(8,128)(2,1)}, bf16[4,128,256]{2,1,0:T(8,128)(2,1)S(1)}, u32[]{:S(2)}) copy-start(bf16[4,128,256]{2,1,0:T(8,128)(2,1)S(1)} %collective-permute-done.refs_0_) | copy-start | bytes 786436
  35.0 34.2 %collective-permute-start.6 = (bf16[4,128,256]{2,1,0:T(8,128)(2,1)}, bf16[4,128,256]{2,1,0:T(8,128)(2,1)S(1)}, u32[]{:S(2)}, u32[]{:S(2)}) collective-permute-start(bf16[4,128,256]{2,1,0:T(8,128)(2,1)} %get-tuple-element.57), channel_id=1, source_target_pairs={{0,101},{1,100},{2,103},{3,102},{4,97},{5,96},{6,99},{7,98},{8,109... | collective-permute-start | bytes 786440 | tf_op jit(solution)/shard_map/ppermute | solution.py:464
  40.5 28.6 %copy-start.17 = (bf16[4,128,256]{2,1,0:T(8,128)(2,1)}, bf16[4,128,256]{2,1,0:T(8,128)(2,1)S(1)}, u32[]{:S(2)}) copy-start(bf16[4,128,256]{2,1,0:T(8,128)(2,1)S(1)} %collective-permute-done.2.refs_4_) | copy-start | bytes 786436
  40.5 28.7 %collective-permute-start.7 = (bf16[4,128,256]{2,1,0:T(8,128)(2,1)}, bf16[4,128,256]{2,1,0:T(8,128)(2,1)S(1)}, u32[]{:S(2)}, u32[]{:S(2)}) collective-permute-start(bf16[4,128,256]{2,1,0:T(8,128)(2,1)} %get-tuple-element.58), channel_id=1, source_target_pairs={{0,102},{1,103},{2,96},{3,97},{4,98},{5,99},{6,100},{7,101},{8,110... | collective-permute-start | bytes 786440 | tf_op jit(solution)/shard_map/ppermute | solution.py:464
  43.2 25.9 %copy-start.18 = (bf16[4,128,256]{2,1,0:T(8,128)(2,1)}, bf16[4,128,256]{2,1,0:T(8,128)(2,1)S(1)}, u32[]{:S(2)}) copy-start(bf16[4,128,256]{2,1,0:T(8,128)(2,1)S(1)} %collective-permute-done.3.refs_1_) | copy-start | bytes 786436
  43.2 26.9 %collective-permute-start.8 = (bf16[4,128,256]{2,1,0:T(8,128)(2,1)}, bf16[4,128,256]{2,1,0:T(8,128)(2,1)S(1)}, u32[]{:S(2)}, u32[]{:S(2)}) collective-permute-start(bf16[4,128,256]{2,1,0:T(8,128)(2,1)} %get-tuple-element.59), channel_id=1, source_target_pairs={{0,103},{1,102},{2,97},{3,96},{4,99},{5,98},{6,101},{7,100},{8,111... | collective-permute-start | bytes 786440 | tf_op jit(solution)/shard_map/ppermute | solution.py:464
  76.1 24.1 %copy-start.7 = (bf16[4,144,256]{2,1,0:T(8,128)(2,1)S(1)}, bf16[4,144,256]{2,1,0:T(8,128)(2,1)}, u32[]{:S(2)}) copy-start(bf16[4,144,256]{2,1,0:T(8,128)(2,1)} %get-tuple-element.68) | copy-start | bytes 884740
  76.1 28.6 %copy-start.8 = (bf16[4,144,256]{2,1,0:T(8,128)(2,1)S(1)}, bf16[4,144,256]{2,1,0:T(8,128)(2,1)}, u32[]{:S(2)}) copy-start(bf16[4,144,256]{2,1,0:T(8,128)(2,1)} %get-tuple-element.69) | copy-start | bytes 884740
  76.1 68.6 %all-to-all-start.2 = ((bf16[8,1024,256]{2,1,0:T(8,128)(2,1)}), bf16[8,1024,256]{2,1,0:T(8,128)(2,1)}, u32[]{:S(2)}, u32[]{:S(2)}) async-start(bf16[8,1024,256]{2,1,0:T(8,128)(2,1)} %routed_pages.2), calls=%async_computation.2 | async-start | bytes 8388608 | tf_op jit(solution)/shard_map/all_to_all | solution.py:524
  80.9 12.0 %collective-permute-start.1 = (bf16[4,144,256]{2,1,0:T(8,128)(2,1)S(1)}, bf16[4,144,256]{2,1,0:T(8,128)(2,1)S(1)}, u32[]{:S(2)}, u32[]{:S(2)}) collective-permute-start(bf16[4,144,256]{2,1,0:T(8,128)(2,1)S(1)} %copy-done.1), channel_id=1, source_target_pairs={{0,96},{1,97},{2,98},{3,99},{4,100},{5,101},{6,102},{7,103},{8,104... | collective-permute-start | bytes 884744 | tf_op jit(solution)/shard_map/ppermute | solution.py:464
  83.6 16.6 %collective-permute-start.9 = (bf16[4,144,256]{2,1,0:T(8,128)(2,1)S(1)}, bf16[4,144,256]{2,1,0:T(8,128)(2,1)S(1)}, u32[]{:S(2)}, u32[]{:S(2)}) collective-permute-start(bf16[4,144,256]{2,1,0:T(8,128)(2,1)S(1)} %copy-done.4), channel_id=1, source_target_pairs={{0,99},{1,98},{2,101},{3,100},{4,103},{5,102},{6,97},{7,96},{8,107... | collective-permute-start | bytes 884744 | tf_op jit(solution)/shard_map/ppermute | solution.py:464
  86.7 18.0 %collective-permute-start.10 = (bf16[4,144,256]{2,1,0:T(8,128)(2,1)S(1)}, bf16[4,144,256]{2,1,0:T(8,128)(2,1)S(1)}, u32[]{:S(2)}, u32[]{:S(2)}) collective-permute-start(bf16[4,144,256]{2,1,0:T(8,128)(2,1)S(1)} %copy-done.2), channel_id=1, source_target_pairs={{0,97},{1,96},{2,99},{3,98},{4,101},{5,100},{6,103},{7,102},{8,105... | collective-permute-start | bytes 884744 | tf_op jit(solution)/shard_map/ppermute | solution.py:464
  88.9 45.4 %collective-permute-start.11 = (bf16[4,144,256]{2,1,0:T(8,128)(2,1)S(1)}, bf16[4,144,256]{2,1,0:T(8,128)(2,1)S(1)}, u32[]{:S(2)}, u32[]{:S(2)}) collective-permute-start(bf16[4,144,256]{2,1,0:T(8,128)(2,1)S(1)} %copy-done.3), channel_id=1, source_target_pairs={{0,98},{1,99},{2,100},{3,101},{4,102},{5,103},{6,96},{7,97},{8,106... | collective-permute-start | bytes 884744 | tf_op jit(solution)/shard_map/ppermute | solution.py:464
  89.4 44.8 %collective-permute-start.12 = (bf16[4,144,256]{2,1,0:T(8,128)(2,1)S(1)}, bf16[4,144,256]{2,1,0:T(8,128)(2,1)}, u32[]{:S(2)}, u32[]{:S(2)}) collective-permute-start(bf16[4,144,256]{2,1,0:T(8,128)(2,1)S(1)} %copy-done.5), channel_id=1, source_target_pairs={{0,100},{1,101},{2,102},{3,103},{4,96},{5,97},{6,98},{7,99},{8,108... | collective-permute-start | bytes 884744 | tf_op jit(solution)/shard_map/ppermute | solution.py:464
  92.9 28.9 %copy-start.9 = (bf16[4,144,256]{2,1,0:T(8,128)(2,1)}, bf16[4,144,256]{2,1,0:T(8,128)(2,1)S(1)}, u32[]{:S(2)}) copy-start(bf16[4,144,256]{2,1,0:T(8,128)(2,1)S(1)} %collective-permute-done.1.refs_0_) | copy-start | bytes 884740
  92.9 41.4 %collective-permute-start.13 = (bf16[4,144,256]{2,1,0:T(8,128)(2,1)S(1)}, bf16[4,144,256]{2,1,0:T(8,128)(2,1)S(1)}, u32[]{:S(2)}, u32[]{:S(2)}) collective-permute-start(bf16[4,144,256]{2,1,0:T(8,128)(2,1)S(1)} %copy-done.6), channel_id=1, source_target_pairs={{0,101},{1,100},{2,103},{3,102},{4,97},{5,96},{6,99},{7,98},{8,109... | collective-permute-start | bytes 884744 | tf_op jit(solution)/shard_map/ppermute | solution.py:464
  100.3 21.5 %copy-start.10 = (bf16[4,144,256]{2,1,0:T(8,128)(2,1)}, bf16[4,144,256]{2,1,0:T(8,128)(2,1)S(1)}, u32[]{:S(2)}) copy-start(bf16[4,144,256]{2,1,0:T(8,128)(2,1)S(1)} %collective-permute-done.9.refs_3_) | copy-start | bytes 884740
  100.3 34.1 %collective-permute-start.14 = (bf16[4,144,256]{2,1,0:T(8,128)(2,1)S(1)}, bf16[4,144,256]{2,1,0:T(8,128)(2,1)S(1)}, u32[]{:S(2)}, u32[]{:S(2)}) collective-permute-start(bf16[4,144,256]{2,1,0:T(8,128)(2,1)S(1)} %copy-done.7), channel_id=1, source_target_pairs={{0,102},{1,103},{2,96},{3,97},{4,98},{5,99},{6,100},{7,101},{8,110... | collective-permute-start | bytes 884744 | tf_op jit(solution)/shard_map/ppermute | solution.py:464
  104.7 17.0 %copy-start.11 = (bf16[4,144,256]{2,1,0:T(8,128)(2,1)}, bf16[4,144,256]{2,1,0:T(8,128)(2,1)S(1)}, u32[]{:S(2)}) copy-start(bf16[4,144,256]{2,1,0:T(8,128)(2,1)S(1)} %collective-permute-done.10.refs_1_) | copy-start | bytes 884740
  104.7 33.7 %collective-permute-start.15 = (bf16[4,144,256]{2,1,0:T(8,128)(2,1)S(1)}, bf16[4,144,256]{2,1,0:T(8,128)(2,1)S(1)}, u32[]{:S(2)}, u32[]{:S(2)}) collective-permute-start(bf16[4,144,256]{2,1,0:T(8,128)(2,1)S(1)} %copy-done.8), channel_id=1, source_target_pairs={{0,103},{1,102},{2,97},{3,96},{4,99},{5,98},{6,101},{7,100},{8,111... | collective-permute-start | bytes 884744 | tf_op jit(solution)/shard_map/ppermute | solution.py:464
  144.7 56.4 %all-to-all-start.1 = ((bf16[8,1088,256]{2,1,0:T(8,128)(2,1)}), bf16[8,1088,256]{2,1,0:T(8,128)(2,1)}, u32[]{:S(2)}, u32[]{:S(2)}) async-start(bf16[8,1088,256]{2,1,0:T(8,128)(2,1)} %routed_pages.3), calls=%async_computation.1 | async-start | bytes 8912896 | tf_op jit(solution)/shard_map/all_to_all | solution.py:524
  (17 other events, 105.2 us)
